TPU v7x, 32 devices: a whole 2x2x4 slice. The times are simulated.
32 devices in a mesh: wide: 8 (over y, x, core), narrow: 4 (over z).
Axes of the slice: x: 2, y: 2, z: 4, core: 2. Of those that a mesh axis runs over, the one named last changes fastest.
Arguments:
- tokens: float32 [18464, 1024], P(('wide', 'narrow')), may hold values from -6 to 6
- cotangent: float32 [18464, 1024], P(('wide', 'narrow')), may hold values from -6 to 6
- triple_weight: float32 [1024, 3, 1024], P('wide', None, 'narrow'), may hold values from -0.1875 to 0.1875
- output_weight: float32 [1024, 1024], P('narrow', 'wide'), may hold values from -2 to 2
- expand_weight: float32 [1024, 4096], P('wide', 'narrow'), may hold values from -0.1875 to 0.1875
- shrink_weight: float32 [4096, 1024], P('narrow', 'wide'), may hold values from -0.09375 to 0.09375
- norm_gains: float32 [2, 1024], replicated, may hold values from 0.5 to 1.5
- shift_biases: float32 [4, 1024], replicated, may hold values from -0.6 to 0.6
- head_biases: float32 [2, 1024], P(None, 'narrow'), may hold values from -0.3 to 0.3
- expand_biases: float32 [4096], P('narrow'), may hold values from -0.6 to 0.6
- triple_first: float32 [1024, 3, 1024], P('wide', None, 'narrow'), may hold values from -89.68232 to 89.68232
- output_first: float32 [1024, 1024], P('narrow', 'wide'), may hold values from -10.59882 to 10.59882
- expand_first: float32 [1024, 4096], P('wide', 'narrow'), may hold values from -27.17646 to 27.17646
- shrink_first: float32 [4096, 1024], P('narrow', 'wide'), may hold values from -51.635273 to 51.635273
- gains_first: float32 [2, 1024], replicated, may hold values from -89.68232 to 89.68232
- shifts_first: float32 [4, 1024], replicated, may hold values from -89.68232 to 89.68232
- heads_first: float32 [2, 1024], P(None, 'narrow'), may hold values from -89.68232 to 89.68232
- widen_first: float32 [4096], P('narrow'), may hold values from -27.17646 to 27.17646
- triple_second: float32 [1024, 3, 1024], P('wide', None, 'narrow'), may hold values from 9.232 to 147.712
- output_second: float32 [1024, 1024], P('narrow', 'wide'), may hold values from 0.147712 to 2.21568
- expand_second: float32 [1024, 4096], P('wide', 'narrow'), may hold values from 0.83088 to 13.29408
- shrink_second: float32 [4096, 1024], P('narrow', 'wide'), may hold values from 3.13888 to 49.8528
- gains_second: float32 [2, 1024], replicated, may hold values from 9.232 to 147.712
- shifts_second: float32 [4, 1024], replicated, may hold values from 9.232 to 147.712
- heads_second: float32 [2, 1024], P(None, 'narrow'), may hold values from 9.232 to 147.712
- widen_second: float32 [4096], P('narrow'), may hold values from 0.83088 to 13.29408
Outputs:
- layer_output: float32 [18464, 1024], P(('wide', 'narrow'))
- input_gradient: float32 [18464, 1024], P(('wide', 'narrow'))
- triple_gradient: float32 [1024, 3, 1024], P('wide', None, 'narrow')
- triple_renewed: float32 [1024, 3, 1024], P('wide', None, 'narrow')
- triple_updated: float32 [1024, 3, 1024], P('wide', None, 'narrow')
- output_gradient: float32 [1024, 1024], P('narrow', 'wide')
- output_renewed: float32 [1024, 1024], P('narrow', 'wide')
- output_updated: float32 [1024, 1024], P('narrow', 'wide')
- expand_gradient: float32 [1024, 4096], P('wide', 'narrow')
- expand_renewed: float32 [1024, 4096], P('wide', 'narrow')
- expand_updated: float32 [1024, 4096], P('wide', 'narrow')
- shrink_gradient: float32 [4096, 1024], P('narrow', 'wide')
- shrink_renewed: float32 [4096, 1024], P('narrow', 'wide')
- shrink_updated: float32 [4096, 1024], P('narrow', 'wide')
- gains_gradient: float32 [2, 1024], replicated
- gains_renewed: float32 [2, 1024], replicated
- gains_updated: float32 [2, 1024], replicated
- shifts_gradient: float32 [4, 1024], replicated
- shifts_renewed: float32 [3, 1024], replicated
- leading_renewed: float32 [1024], replicated
- shifts_updated: float32 [4, 1024], replicated
- heads_gradient: float32 [2, 1024], P(None, 'narrow')
- heads_renewed: float32 [2, 1024], P(None, 'narrow')
- heads_updated: float32 [2, 1024], P(None, 'narrow')
- widen_gradient: float32 [4096], P('narrow')
- widen_renewed: float32 [4096], P('narrow')
- widen_updated: float32 [4096], P('narrow')
All inputs are finite; a program needn't handle non-finite values.
Results may differ from a plain program's by a relative error of at most 0.019.
Values may be sent and summed in bfloat16 or wider, within the bound.
No kernel may reach another device: no remote copies, remote signals or barrier semaphores. Data moves between devices by JAX's collectives and lax.ppermute only.
A program may use at most 192 MiB of HBM per device.

v0:
```python
import functools
import math

import jax
import jax.numpy as jnp
from jax import lax
from jax.experimental import pallas as pl
from jax.experimental.pallas import tpu as pltpu
from jax.sharding import PartitionSpec as P

D = 1024
H = 16
SEQ = 577
STEP = 10
HEAD = D // H
LANES = 128
BLOCKS = D // LANES
HALF = D // 2


norm_eps = 1e-06
beta_first = 0.9
beta_second = 0.999
adam_eps = 1e-08
decay_rate = 0.05

low = jnp.bfloat16
full = jnp.float32
big = pltpu.CompilerParams(vmem_limit_bytes=56 * 1024 * 1024)


def adam_step(weight, grad, first, second, rate, decay):
    first_new = beta_first * first + (1.0 - beta_first) * grad
    second_new = beta_second * second + (1.0 - beta_second) * grad * grad
    first_hat = first_new / (1.0 - beta_first**STEP)
    second_hat = second_new / (1.0 - beta_second**STEP)
    updated = weight - rate * (first_hat / (jnp.sqrt(second_hat) + adam_eps) + decay * weight)
    return (second_new, updated)


def dot_nn(left, right):
    return lax.dot_general(left, right, (((1,), (0,)), ((), ())), preferred_element_type=full)


def dot_nt(left, right):
    return lax.dot_general(left, right, (((1,), (1,)), ((), ())), preferred_element_type=full)


def dot_tn(left, right):
    return lax.dot_general(left, right, (((0,), (0,)), ((), ())), preferred_element_type=full)


def lane_block(order, at):
    return pl.ds(pl.multiple_of(order[at] * LANES, LANES), LANES)


def stat(values):
    center = values - jnp.mean(values, axis=-1, keepdims=True)
    inverse = lax.rsqrt(jnp.mean(center * center, axis=-1, keepdims=True) + norm_eps)
    return center * inverse, inverse


def norm_back(values, grad, gain):
    unit, inverse = stat(values)
    scaled = grad * gain
    part = inverse * (
        scaled
        - jnp.mean(scaled, axis=-1, keepdims=True)
        - unit * jnp.mean(scaled * unit, axis=-1, keepdims=True)
    )
    gain_sum = jnp.sum(grad * unit, axis=0, keepdims=True)
    shift_sum = jnp.sum(grad, axis=0, keepdims=True)
    return part, gain_sum, shift_sum


def start_kernel(order, tok, cot, gains, shifts, tok_out, normed, cot_out, cot_low, gains_out, shifts_out, cot_sum):
    values = tok[...]
    mean = jnp.mean(values, axis=-1, keepdims=True)
    center = values - mean
    inverse = lax.rsqrt(jnp.mean(center * center, axis=-1, keepdims=True) + norm_eps)
    cot_sum[...] = jnp.sum(cot[...], axis=0, keepdims=True)
    for at in range(BLOCKS):
        source = lane_block(order, at)
        place = slice(at * LANES, (at + 1) * LANES)
        block = tok[:, source]
        tok_out[:, place] = block
        gain = gains[:, source]
        shift = shifts[:, source]
        gains_out[:, place] = gain
        shifts_out[:, place] = shift
        normed[:, place] = ((block - mean) * inverse * gain[0:1] + shift[0:1]).astype(low)
        other = cot[:, source]
        cot_out[:, place] = other
        cot_low[:, place] = other.astype(low)


def piece_specs(pieces, width, lane=0):
    groups = pieces[0].shape[0]
    cut = groups // 2
    shape = (1, pieces[0].shape[1], width)
    same = pl.BlockSpec(shape, lambda n, *s: (n, 0, lane))
    first = pl.BlockSpec(shape, lambda n, *s: (jnp.minimum(n, cut - 1), 0, lane))
    second = pl.BlockSpec(shape, lambda n, *s: (jnp.maximum(n - cut, 0), 0, lane))
    return [same, same, same, first, second]


def assemble(refs, groups):
    near = [ref[0] for ref in refs[:3]]
    far = jnp.where(pl.program_id(0) < groups // 2, refs[3][0], refs[4][0])
    return jnp.concatenate(near + [far], axis=0)


def whole_spec(*shape):
    return pl.BlockSpec(shape, lambda n, *s: (0,) * len(shape))


def once_spec(*shape):
    return pl.BlockSpec(shape, lambda n, *s: (0,) * len(shape), pipeline_mode=pl.Buffered(1))


def twin_half(rows):
    return pl.BlockSpec((rows, HALF), lambda n, *s: (0, 1), pipeline_mode=pl.Buffered(1))


def group_spec(*shape):
    return pl.BlockSpec((1,) + shape, lambda n, *s: (n,) + (0,) * len(shape))


def grouped(kernel, groups, ins, outs, out_shapes, args, scratch=(), prefetch=0):
    return pl.pallas_call(
        kernel,
        grid_spec=pltpu.PrefetchScalarGridSpec(
            num_scalar_prefetch=prefetch,
            grid=(groups,),
            in_specs=ins,
            out_specs=outs,
            scratch_shapes=list(scratch),
        ),
        out_shape=out_shapes,
        compiler_params=big,
    )(*args)


def struct(shape, dtype):
    return jax.ShapeDtypeStruct(shape, dtype)


def attend_kernel(groups, *refs):
    x, bias = refs[:2]
    own, twin = refs[2:7], refs[7:12]
    packed, mixed, logs = refs[12:]
    value = dot_nn(x[:, :HALF], assemble(own, groups)) + dot_nn(x[:, HALF:], assemble(twin, groups)) + bias[0]
    width = value.shape[1] // 3
    value = value.astype(low)
    packed[0] = value
    lane = lax.broadcasted_iota(jnp.int32, (1, LANES), 1)
    scale = 1.0 / math.sqrt(HEAD)
    rows = value.shape[0]
    log_all = jnp.zeros((rows, LANES), full)
    for pair in range(width // LANES):
        cols = slice(pair * LANES, (pair + 1) * LANES)
        query = value[:, cols]
        key = value[:, width + pair * LANES : width + (pair + 1) * LANES]
        val = value[:, 2 * width + pair * LANES : 2 * width + (pair + 1) * LANES]
        outs = []
        for side in range(2):
            keep = jnp.where(lane // HEAD == side, scale, 0.0).astype(low)
            scores = dot_nt(query * keep, key)
            top = jnp.max(scores, axis=-1, keepdims=True)
            expon = jnp.exp(scores - top)
            total = jnp.sum(expon, axis=-1, keepdims=True)
            outs.append(dot_nn(expon.astype(low), val) / total)
            log_all = jnp.where(lane == 2 * pair + side, top + jnp.log(total), log_all)
        mixed[0, :, cols] = jnp.where(lane < HEAD, outs[0], outs[1]).astype(low)
    logs[0] = log_all.T[:8]


def attend(normed, bias, own, twin):
    groups, _, width = bias.shape
    rows = normed.shape[0]
    return grouped(
        functools.partial(attend_kernel, groups),
        groups,
        [whole_spec(rows, D), group_spec(1, width)] + piece_specs(own, width) + piece_specs(twin, width),
        [group_spec(rows, width), group_spec(rows, width // 3), group_spec(8, rows)],
        [struct((groups, rows, width), low), struct((groups, rows, width // 3), low), struct((groups, 8, rows), full)],
        (normed, bias, *own, *twin),
    )


def attend_back_kernel(groups, *refs):
    grad, packed, logs, normed = refs[:4]
    own, twin = refs[4:9], refs[9:14]
    out, sums, outer = refs[14:]
    upper = (dot_nn(grad[:, :HALF], assemble(own, groups)) + dot_nn(grad[:, HALF:], assemble(twin, groups))).astype(low)
    width = upper.shape[1]
    lane = lax.broadcasted_iota(jnp.int32, (1, LANES), 1)
    scale = 1.0 / math.sqrt(HEAD)
    for pair in range(width // LANES):
        cols = slice(pair * LANES, (pair + 1) * LANES)
        query = packed[0, :, cols]
        key = packed[0, :, width + pair * LANES : width + (pair + 1) * LANES]
        val = packed[0, :, 2 * width + pair * LANES : 2 * width + (pair + 1) * LANES]
        up = upper[:, cols]
        parts = []
        for side in range(2):
            head = 2 * pair + side
            inside = lane // HEAD == side
            scores = dot_nt(key * jnp.where(inside, scale, 0.0).astype(low), query)
            probs = jnp.exp(scores - logs[0, head : head + 1, :])
            val_grad = dot_nn(probs.astype(low), up)
            prob_grad = dot_nt(val * jnp.where(inside, 1.0, 0.0).astype(low), up)
            weighted = probs * prob_grad
            score_grad = (weighted - probs * jnp.sum(weighted, axis=0, keepdims=True)).astype(low)
            key_grad = dot_nn(score_grad, query) * scale
            query_grad = dot_tn(score_grad, key) * scale
            parts.append((query_grad, key_grad, val_grad))
        for kind in range(3):
            both = jnp.where(lane < HEAD, parts[0][kind], parts[1][kind])
            start = kind * width + pair * LANES
            out[0, :, start : start + LANES] = both.astype(low)
            if kind != 1:
                sums[0, kind // 2 : kind // 2 + 1, cols] = jnp.sum(both, axis=0, keepdims=True)
    outer[0] = dot_tn(normed[...], out[0]).astype(low)


def attend_back(grad, packed, logs, normed, own, twin, lane):
    groups, rows, width = packed.shape
    third = width // 3
    return grouped(
        functools.partial(attend_back_kernel, groups),
        groups,
        [whole_spec(rows, D), group_spec(rows, width), group_spec(8, rows), twin_half(rows)]
        + piece_specs(own, third, lane)
        + piece_specs(twin, third, lane),
        [group_spec(rows, width), group_spec(2, third), group_spec(HALF, width)],
        [
            struct((groups, rows, width), low),
            struct((groups, 2, third), full),
            struct((groups, HALF, width), low),
        ],
        (grad, packed, logs, normed, *own, *twin),
    )


def add_parts(groups, inner, own, twin, total):
    total[:, :HALF] += dot_nt(inner[0], assemble(own, groups))
    total[:, HALF:] += dot_nt(inner[0], assemble(twin, groups))


def middle_kernel(groups, *refs):
    mixed, tok, gains, shifts = refs[:4]
    own, twin = refs[4:9], refs[9:14]
    middle, normed, total = refs[14:]
    n = pl.program_id(0)

    @pl.when(n == 0)
    def _():
        total[...] = tok[...] + shifts[2:3]

    add_parts(groups, mixed, own, twin, total)

    @pl.when(n == groups - 1)
    def _():
        values = total[...]
        middle[...] = values
        unit, _ = stat(values)
        normed[...] = (unit * gains[1:2] + shifts[1:2]).astype(low)


def middle_call(mixed, tok, gains, shifts, own, twin, lane):
    groups, rows, width = mixed.shape
    return grouped(
        functools.partial(middle_kernel, groups),
        groups,
        [group_spec(rows, width), whole_spec(rows, D), whole_spec(2, D), whole_spec(4, D)]
        + piece_specs(own, width, lane)
        + piece_specs(twin, width, lane),
        [whole_spec(rows, D), whole_spec(rows, D)],
        [struct((rows, D), full), struct((rows, D), low)],
        (mixed, tok, gains, shifts, *own, *twin),
        scratch=[pltpu.VMEM((rows, D), full)],
    )


def expand_kernel(groups, *refs):
    x, bias, cot = refs[:3]
    own, twin = refs[3:8], refs[8:13]
    active, slope, outer = refs[13:]
    value = dot_nn(x[:, :HALF], assemble(own, groups)) + dot_nn(x[:, HALF:], assemble(twin, groups)) + bias[0]
    phi = 0.5 * (1.0 + lax.erf(value * math.sqrt(0.5)))
    low_active = (value * phi).astype(low)
    active[0] = low_active
    outer[0] = dot_tn(cot[...], low_active).astype(low)
    slope[0] = (phi + value * (jnp.exp(-0.5 * value * value) * (1.0 / math.sqrt(2.0 * math.pi)))).astype(low)


def expand(normed, bias, cot, own, twin):
    groups, rows, width = bias.shape[0], normed.shape[0], bias.shape[2]
    shape = struct((groups, rows, width), low)
    return grouped(
        functools.partial(expand_kernel, groups),
        groups,
        [whole_spec(rows, D), group_spec(1, width), twin_half(rows)]
        + piece_specs(own, width)
        + piece_specs(twin, width),
        [group_spec(rows, width)] * 2 + [group_spec(HALF, width)],
        [shape, shape, struct((groups, HALF, width), low)],
        (normed, bias, cot, *own, *twin),
    )


def hidden_back_kernel(groups, order, *refs):
    grad, slope, active, middle, cot, gains, shifts, normed = refs[:8]
    shrink_own, shrink_twin = refs[8:13], refs[13:18]
    expand_own, expand_twin = refs[18:23], refs[23:28]
    inner, sums, outer, layer, out, out_low, two_sums, total, result = refs[28:]
    n = pl.program_id(0)

    @pl.when(n == 0)
    def _():
        total[...] = jnp.zeros_like(total)
        result[...] = middle[...] + shifts[3:4]

    own, twin = assemble(shrink_own, groups), assemble(shrink_twin, groups)
    value = (dot_nn(grad[:, :HALF], own) + dot_nn(grad[:, HALF:], twin)) * slope[0].astype(full)
    sums[0] = jnp.sum(value, axis=0, keepdims=True)
    low_value = value.astype(low)
    inner[0] = low_value
    result[:, :HALF] += dot_nt(active[0], own)
    result[:, HALF:] += dot_nt(active[0], twin)
    outer[0] = dot_tn(normed[...], low_value).astype(low)
    add_parts(groups, inner, expand_own, expand_twin, total)

    @pl.when(n == groups - 1)
    def _():
        part, gain_sum, shift_sum = norm_back(middle[...], total[...], gains[1:2])
        grad_out = cot[...] + part
        out[...] = grad_out
        out_low[...] = grad_out.astype(low)
        grad_sum = jnp.sum(grad_out, axis=0, keepdims=True)
        for at in range(BLOCKS):
            place = lane_block(order, at)
            cols = slice(at * LANES, (at + 1) * LANES)
            layer[:, place] = result[:, cols]
            two_sums[0:1, place] = gain_sum[:, cols]
            two_sums[1:2, place] = shift_sum[:, cols]
            two_sums[2:3, place] = grad_sum[:, cols]


def hidden_back(order, grad, slope, active, middle, cot, gains, shifts, normed, shrink_own, shrink_twin, own, twin):
    groups, rows, width = slope.shape
    group = group_spec(rows, width)
    pieces = piece_specs(own, width)
    once = once_spec(rows, D)
    return grouped(
        functools.partial(hidden_back_kernel, groups),
        groups,
        [once, group, group, once, once, whole_spec(2, D), whole_spec(4, D), twin_half(rows)] + pieces * 4,
        [group, group_spec(1, width), group_spec(HALF, width), once, once, once, whole_spec(3, D)],
        [
            struct((groups, rows, width), low),
            struct((groups, 1, width), full),
            struct((groups, HALF, width), low),
            struct((rows, D), full),
            struct((rows, D), full),
            struct((rows, D), low),
            struct((3, D), full),
        ],
        (
            order,
            grad,
            slope,
            active,
            middle,
            cot,
            gains,
            shifts,
            normed,
            *shrink_own,
            *shrink_twin,
            *own,
            *twin,
        ),
        scratch=[pltpu.VMEM((rows, D), full), pltpu.VMEM((rows, D), full)],
        prefetch=1,
    )


def outer_twin_kernel(x, inner, out):
    out[0] = dot_tn(x[...], inner[0]).astype(low)


def outer_twin(x, inner):
    groups, rows, width = inner.shape
    return grouped(
        outer_twin_kernel,
        groups,
        [pl.BlockSpec((rows, HALF), lambda n: (0, 1)), group_spec(rows, width)],
        group_spec(HALF, width),
        struct((groups, HALF, width), low),
        (x, inner),
    )


def outer_own_kernel(groups, x, inner, other, mine, to_x, to_y, far_first, far_second):
    value = (dot_tn(x[...], inner[0]) + other[0].astype(full)).astype(low)
    rows = HALF // 4
    mine[0] = value[:rows]
    to_x[0] = value[rows : 2 * rows]
    to_y[0] = value[2 * rows : 3 * rows]
    n = pl.program_id(0)

    @pl.when(n < groups // 2)
    def _():
        far_first[0] = value[3 * rows :]

    @pl.when(n >= groups // 2)
    def _():
        far_second[0] = value[3 * rows :]


def outer_own(x, inner, other):
    groups, rows, width = inner.shape
    near = struct((groups, HALF // 4, width), low)
    far = struct((groups // 2, HALF // 4, width), low)
    shapes = [near, near, near, far, far]
    return grouped(
        functools.partial(outer_own_kernel, groups),
        groups,
        [pl.BlockSpec((rows, HALF), lambda n: (0, 0)), group_spec(rows, width), group_spec(HALF, width)],
        piece_specs(shapes, width),
        shapes,
        (x, inner, other),
    )


def norm_one_kernel(groups, order, *refs):
    inner, tok, grad, gains = refs[:4]
    own, twin = refs[4:9], refs[9:14]
    out, sums, total = refs[14:]
    n = pl.program_id(0)

    @pl.when(n == 0)
    def _():
        total[...] = jnp.zeros_like(total)

    add_parts(groups, inner, own, twin, total)

    @pl.when(n == groups - 1)
    def _():
        part, gain_sum, shift_sum = norm_back(tok[...], total[...], gains[0:1])
        result = grad[...] + part
        for at in range(BLOCKS):
            place = lane_block(order, at)
            cols = slice(at * LANES, (at + 1) * LANES)
            out[:, place] = result[:, cols]
            sums[0:1, place] = gain_sum[:, cols]
            sums[1:2, place] = shift_sum[:, cols]


def norm_one(order, inner, values, grad, gains, own, twin):
    groups, rows, width = inner.shape
    whole = whole_spec(rows, D)
    return grouped(
        functools.partial(norm_one_kernel, groups),
        groups,
        [group_spec(rows, width), whole, whole, whole_spec(2, D)] + piece_specs(own, width) + piece_specs(twin, width),
        [whole, whole_spec(2, D)],
        [struct((rows, D), full), struct((2, D), full)],
        (order, inner, values, grad, gains, *own, *twin),
        scratch=[pltpu.VMEM((rows, D), full)],
        prefetch=1,
    )


def swap(values, bit):
    return lax.ppermute(values, "wide", [(at, at ^ bit) for at in range(8)])


def turn(values, step):
    return lax.ppermute(values, "narrow", [(at, (at + step) % 4) for at in range(4)])


def cross(values, bit):
    return lax.ppermute(values, "narrow", [(at, at ^ bit) for at in range(4)])


def fence(*values):
    return lax.optimization_barrier(values)


def plain_gather(block):
    groups = lax.all_gather(block, "narrow", axis=0, tiled=False)
    whole = lax.all_gather(groups, "wide", axis=1, tiled=True)
    rows, cut = HALF // 4, whole.shape[0] // 2
    sides = []
    for side in range(2):
        parts = [whole[:, side * HALF + at * rows : side * HALF + (at + 1) * rows] for at in range(4)]
        sides.append((*parts[:3], parts[3][:cut], parts[3][cut:]))
    return tuple(sides)


def plain_scatter(pieces, twin):
    far = jnp.concatenate(pieces[3:], axis=0)
    whole = jnp.concatenate([*pieces[:3], far, twin], axis=1)
    part = lax.psum_scatter(whole, "wide", scatter_dimension=1, tiled=True)
    return lax.psum_scatter(part, "narrow", scatter_dimension=0, tiled=False).astype(full)


def around(block):
    return [turn(block, step) for step in range(1, 4)]


def near_sends(pieces, from_y, from_x):
    cut = from_y.shape[0]
    to_x = jnp.concatenate([(pieces[1][:cut].astype(full) + from_y.astype(full)).astype(low), pieces[1][cut:]], axis=0)
    to_y = jnp.concatenate([pieces[2][:cut], (pieces[2][cut:].astype(full) + from_x.astype(full)).astype(low)], axis=0)
    return to_x, to_y


def last_sends(mine, over_x, over_y):
    part = (mine.astype(full) + over_x.astype(full) + over_y.astype(full)).astype(low)
    return tuple(part[at] for at in range(4))


def narrow_scatter(mine, over_x, over_y, places):
    part = (mine.astype(full) + over_x.astype(full) + over_y.astype(full)).astype(low)
    parts = [lax.dynamic_index_in_dim(part, places[at], 0, keepdims=False) for at in range(4)]
    return lax.psum_scatter(jnp.stack(parts), "narrow", scatter_dimension=0, tiled=False).astype(full)


def last_sum(first, rest):
    total = first.astype(full)
    for part in rest:
        total = total + part.astype(full)
    return total


def shards(
    tokens,
    cotangent,
    triple_weight,
    output_weight,
    expand_weight,
    shrink_weight,
    norm_gains,
    shift_biases,
    head_biases,
    expand_biases,
    triple_first,
    output_first,
    expand_first,
    shrink_first,
    gains_first,
    shifts_first,
    heads_first,
    widen_first,
    triple_second,
    output_second,
    expand_second,
    shrink_second,
    gains_second,
    shifts_second,
    heads_second,
    widen_second,
    *,
    wide,
    narrow,
):
    tuned = wide == 8 and narrow == 4
    rows = tokens.shape[0]
    local = head_biases.shape[1]
    hidden = expand_biases.shape[0]
    place = lax.axis_index("wide")
    at_narrow = lax.axis_index("narrow")
    if tuned:
        order = jnp.bitwise_xor(place, jnp.array([0, 2, 4, 6, 1, 3, 5, 7], jnp.int32)).astype(jnp.int32)
        group_order = (at_narrow - jnp.arange(narrow)) % narrow
    else:
        order = jnp.arange(BLOCKS, dtype=jnp.int32)
        group_order = jnp.arange(narrow)

    triple_block = jnp.concatenate([triple_weight[:, at].astype(low) for at in range(3)] + [output_weight.astype(low).T], axis=1)
    expand_block = expand_weight.astype(low)
    shrink_block = shrink_weight.astype(low).T
    bias_block = jnp.concatenate([head_biases[0], head_biases[1], expand_biases])

    def begin(order, tokens, cotangent):
        return pl.pallas_call(
            start_kernel,
            in_specs=[pl.BlockSpec(memory_space=pltpu.SMEM)] + [pl.BlockSpec(memory_space=pltpu.VMEM)] * 4,
            out_shape=[
                struct((rows, D), full),
                struct((rows, D), low),
                struct((rows, D), full),
                struct((rows, D), low),
                struct((2, D), full),
                struct((4, D), full),
                struct((1, D), full),
            ],
            compiler_params=big,
        )(order, tokens, cotangent, norm_gains, shift_biases)

    def split_bias(biases):
        triple_bias = jnp.concatenate(
            [biases[:, :local], jnp.zeros((narrow, local), full), biases[:, local : 2 * local]], axis=1
        )
        return triple_bias[:, None], biases[:, 2 * local :][:, None]

    if tuned:
        triple_turns = around(triple_block)
        begun = begin(order, tokens, cotangent)
        triple_turns, begun, triple_block, expand_block, shrink_block, bias_block = fence(
            triple_turns, begun, triple_block, expand_block, shrink_block, bias_block
        )
        tok, normed, cot, cot_low, gains, shifts, cot_sum = begun
        t_near = jnp.stack([triple_block, *triple_turns])
        t_x, t_y = swap(t_near, 2), swap(t_near, 4)
        expand_turns = around(expand_block)
        t_near, t_x, t_y, expand_turns, expand_block, normed, bias_block = fence(
            t_near, t_x, t_y, expand_turns, expand_block, normed, bias_block
        )
        t_f, t_g = swap(t_x[:2], 4), swap(t_y[2:], 2)
        t_near_c, t_x_c, t_y_c = swap(t_near, 1), swap(t_x, 1), swap(t_y, 1)
        e_near = jnp.stack([expand_block, *expand_turns])
        t_f, t_g, t_near_c, t_x_c, t_y_c, e_near, normed, bias_block, shrink_block = fence(
            t_f, t_g, t_near_c, t_x_c, t_y_c, e_near, normed, bias_block, shrink_block
        )
        e_x, e_y = swap(e_near, 2), swap(e_near, 4)
        t_f_c, t_g_c = swap(t_f, 1), swap(t_g, 1)
        triple_own = (t_near, t_x, t_y, t_f, t_g)
        triple_twin = (t_near_c, t_x_c, t_y_c, t_f_c, t_g_c)
        bias_turns = around(bias_block)
        triple_twin, bias_turns, normed, shrink_block = fence(triple_twin, bias_turns, normed, shrink_block)
        triple_bias, widen_bias = split_bias(jnp.stack([bias_block, *bias_turns]))
        shrink_turns = around(shrink_block)
        packed, mixed, logs = attend(normed, triple_bias, triple_own, triple_twin)
        e_near, e_x, e_y, mixed, shrink_turns, shrink_block, tok = fence(
            e_near, e_x, e_y, mixed, shrink_turns, shrink_block, tok
        )
        e_f, e_g = swap(e_x[:2], 4), swap(e_y[2:], 2)
        e_near_c, e_x_c, e_y_c = swap(e_near, 1), swap(e_x, 1), swap(e_y, 1)
        middle, normed_two = middle_call(mixed, tok, gains, shifts, triple_own, triple_twin, 3)
        s_near = jnp.stack([shrink_block, *shrink_turns])
        e_f, e_g, e_near_c, e_x_c, e_y_c, s_near, normed_two = fence(
            e_f, e_g, e_near_c, e_x_c, e_y_c, s_near, normed_two
        )
        s_x, s_y = swap(s_near, 2), swap(s_near, 4)
        expand_own = (e_near, e_x, e_y, e_f, e_g)
        expand_twin = (e_near_c, e_x_c, e_y_c, swap(e_f, 1), swap(e_g, 1))
    else:
        tok, normed, cot, cot_low, gains, shifts, cot_sum = begin(order, tokens, cotangent)
        triple_bias, widen_bias = split_bias(lax.all_gather(bias_block, "narrow", axis=0, tiled=False))
        triple_own, triple_twin = plain_gather(triple_block)
        expand_own, expand_twin = plain_gather(expand_block)
        shrink_own, shrink_twin = plain_gather(shrink_block)
        packed, mixed, logs = attend(normed, triple_bias, triple_own, triple_twin)
        middle, normed_two = middle_call(mixed, tok, gains, shifts, triple_own, triple_twin, 3)

    active, slope, s_twin = expand(normed_two, widen_bias, cot_low, expand_own, expand_twin)
    if tuned:
        s_near, s_x, s_y, s_twin, cot_low, active = fence(s_near, s_x, s_y, s_twin, cot_low, active)
        s_f, s_g = swap(s_x[:2], 4), swap(s_y[2:], 2)
        s_other = swap(s_twin, 1)
        s_near_c, s_x_c = swap(s_near, 1), swap(s_x, 1)
        s_pieces = outer_own(cot_low, active, s_other)
        s_f, s_g, s_pieces, s_near_c, s_x_c, cot_low, slope = fence(
            s_f, s_g, s_pieces, s_near_c, s_x_c, cot_low, slope
        )
        from_y, from_x = swap(s_pieces[3], 4), swap(s_pieces[4], 2)
        shrink_own = (s_near, s_x, s_y, s_f, s_g)
        shrink_twin = (s_near_c, s_x_c, swap(s_y, 1), swap(s_f, 1), swap(s_g, 1))
    else:
        s_pieces = outer_own(cot_low, active, jnp.zeros_like(s_twin))
    expanded_low, widen_sum, e_twin, layer_output, middle_grad, middle_low, two_sums = hidden_back(
        order,
        cot_low,
        slope,
        active,
        middle,
        cot,
        gains,
        shifts,
        normed_two,
        shrink_own,
        shrink_twin,
        expand_own,
        expand_twin,
    )
    if tuned:
        from_y, from_x, expanded_low, e_twin, s_pieces = fence(from_y, from_x, expanded_low, e_twin, s_pieces)
        e_other = swap(e_twin, 1)
        to_x, to_y = near_sends(s_pieces, from_y, from_x)
        s_over_x, s_over_y = swap(to_x, 2), swap(to_y, 4)
    else:
        e_other = jnp.zeros_like(e_twin)
    e_pieces = outer_own(normed_two, expanded_low, e_other)
    if tuned:
        e_pieces, middle_low, packed = fence(e_pieces, middle_low, packed)
        from_y, from_x = swap(e_pieces[3], 4), swap(e_pieces[4], 2)
    triple_low, head_sums, t_twin = attend_back(middle_low, packed, logs, normed, triple_own, triple_twin, 3)
    if tuned:
        from_y, from_x, s_over_x, s_over_y, t_twin, triple_low, e_pieces, s_pieces, mixed = fence(
            from_y, from_x, s_over_x, s_over_y, t_twin, triple_low, e_pieces, s_pieces, mixed
        )
        t_other = swap(t_twin, 1)
        to_x, to_y = near_sends(e_pieces, from_y, from_x)
        e_over_x, e_over_y = swap(to_x, 2), swap(to_y, 4)
        o_twin = outer_twin(middle_low, mixed)
        t_other, o_twin, triple_low, normed = fence(t_other, o_twin, triple_low, normed)
    else:
        t_other = jnp.zeros_like(t_twin)
        o_twin = outer_twin(middle_low, mixed)
    t_pieces = outer_own(normed, triple_low, t_other)
    if tuned:
        t_pieces, o_twin, triple_low = fence(t_pieces, o_twin, triple_low)
        t_from_y, t_from_x = swap(t_pieces[3], 4), swap(t_pieces[4], 2)
        o_other = swap(o_twin, 1)
        shrink_grad = narrow_scatter(s_pieces[0], s_over_x, s_over_y, group_order)
    else:
        o_other = jnp.zeros_like(o_twin)
    input_gradient, one_sums = norm_one(
        order, triple_low, tok, middle_grad, gains, triple_own, triple_twin
    )
    small = jnp.concatenate(
        [
            one_sums[0:1],
            two_sums[0:1],
            one_sums[1:2],
            two_sums[1:3],
            cot_sum,
            head_sums[group_order].transpose(1, 0, 2).reshape(2, D),
            widen_sum[group_order].reshape(-1, D),
        ],
        axis=0,
    )
    o_pieces = outer_own(middle_low, mixed, o_other)
    if tuned:
        t_from_y, t_from_x, small, t_pieces, e_over_x, e_over_y, o_pieces, shrink_grad = fence(
            t_from_y, t_from_x, small, t_pieces, e_over_x, e_over_y, o_pieces, shrink_grad
        )
        to_x, to_y = near_sends(t_pieces, t_from_y, t_from_x)
        t_over_x, t_over_y = swap(to_x, 2), swap(to_y, 4)
        expand_gradient = narrow_scatter(e_pieces[0], e_over_x, e_over_y, group_order)
        from_y, from_x = swap(o_pieces[3], 4), swap(o_pieces[4], 2)
        to_x, to_y = near_sends(o_pieces, from_y, from_x)
        o_over_x, o_over_y = swap(to_x, 2), swap(to_y, 4)
        small = small + swap(small, 1)
        small = small + cross(small, 1)
        small = small + cross(small, 2)
        small = small + swap(small, 2)
        small = small + swap(small, 4)
        t_over_x, t_over_y, o_over_x, o_over_y, small, expand_gradient = fence(
            t_over_x, t_over_y, o_over_x, o_over_y, small, expand_gradient
        )
        t_last = last_sends(t_pieces[0], t_over_x, t_over_y)
        t_back = [turn(t_last[step], -step) for step in range(1, 4)]
        output_grad = narrow_scatter(o_pieces[0], o_over_x, o_over_y, group_order)
        triple_grad = last_sum(t_last[0], t_back)
    else:
        small = lax.psum(small, ("wide", "narrow"))
        triple_grad = plain_scatter(t_pieces, t_twin)
        output_grad = plain_scatter(o_pieces, o_twin)
        expand_gradient = plain_scatter(e_pieces, e_twin)
        shrink_grad = plain_scatter(s_pieces, s_twin)
    triple_gradient = jnp.stack([triple_grad[:, at * local : (at + 1) * local] for at in range(3)], axis=1)
    output_gradient = output_grad.T
    shrink_gradient = shrink_grad.T
    gains_gradient = small[0:2]
    shifts_gradient = small[2:6]
    heads_gradient = lax.dynamic_slice_in_dim(small[6:8], at_narrow * local, local, 1)
    widen_gradient = lax.dynamic_slice_in_dim(small[8:].reshape(-1), at_narrow * hidden, hidden, 0)

    params = (
        triple_weight,
        output_weight,
        expand_weight,
        shrink_weight,
        norm_gains,
        shift_biases,
        head_biases,
        expand_biases,
    )
    gradients = (
        triple_gradient,
        output_gradient,
        expand_gradient,
        shrink_gradient,
        gains_gradient,
        shifts_gradient,
        heads_gradient,
        widen_gradient,
    )
    firsts = (
        triple_first,
        output_first,
        expand_first,
        shrink_first,
        gains_first,
        shifts_first,
        heads_first,
        widen_first,
    )
    seconds = (
        triple_second,
        output_second,
        expand_second,
        shrink_second,
        gains_second,
        shifts_second,
        heads_second,
        widen_second,
    )
    rates = (0.1, 1.0, 0.1, 0.05, 1.0, 0.3, 0.2, 0.3)
    decays = (decay_rate, decay_rate, decay_rate, decay_rate, 0.0, 0.0, 0.0, 0.0)
    results = [layer_output, input_gradient]
    for index in range(8):
        renewed, updated = adam_step(
            params[index],
            gradients[index],
            firsts[index],
            seconds[index],
            rates[index],
            decays[index],
        )
        if index == 5:
            results.extend([gradients[index], renewed[1:], renewed[0], updated])
        else:
            results.extend([gradients[index], renewed, updated])
    return tuple(results)


def solution(mesh):
    placed = (
        P(("wide", "narrow"), None),
        P(("wide", "narrow"), None),
        P("wide", None, "narrow"),
        P("narrow", "wide"),
        P("wide", "narrow"),
        P("narrow", "wide"),
        P(),
        P(),
        P(None, "narrow"),
        P("narrow"),
        P("wide", None, "narrow"),
        P("narrow", "wide"),
        P("wide", "narrow"),
        P("narrow", "wide"),
        P(),
        P(),
        P(None, "narrow"),
        P("narrow"),
        P("wide", None, "narrow"),
        P("narrow", "wide"),
        P("wide", "narrow"),
        P("narrow", "wide"),
        P(),
        P(),
        P(None, "narrow"),
        P("narrow"),
    )
    matrices = (P("wide", None, "narrow"), P("narrow", "wide"), P("wide", "narrow"), P("narrow", "wide"))
    outs = [P(("wide", "narrow"), None), P(("wide", "narrow"), None)]
    for spec in matrices:
        outs.extend([spec] * 3)
    outs.extend([P()] * 7)
    outs.extend([P(None, "narrow")] * 3)
    outs.extend([P("narrow")] * 3)
    return jax.shard_map(
        functools.partial(shards, wide=mesh.shape["wide"], narrow=mesh.shape["narrow"]),
        mesh=mesh,
        in_specs=placed,
        out_specs=tuple(outs),
        check_vma=False,
    )
```

profile of v0, /device:TPU:0, one launch (start us, length us, event | category | flops | bytes accessed | tf_op | source)
XLA Modules:
  0.0 412.7 jit_solution(9517789129507098190)
XLA Ops:
  19.4 7.0 %shard_map.466 = (f32[577,1024]{1,0:T(8,128)}, bf16[577,1024]{1,0:T(8,128)(2,1)}, f32[577,1024]{1,0:T(8,128)}, bf16[577,1024]{1,0:T(8,128)(2,1)}, f32[2,1024]{1,...) custom-call(s32[8]{0:T(128)} %broadcast_xor_fusion.order, f32[577,1024]{1,0:T(8,128)} %tok.1, f32[577,1024]{1,0:T(8,128)} %cot.1, ...), custom_call_target="tpu_custom_call" | custom-call | tf_op jit(solution)/shard_map/pallas_call | solution.py:590
  26.4 5.8 %collective-permute-done.1 = bf16[128,1024]{1,0:T(8,128)(2,1)S(1)} collective-permute-done((bf16[128,1024]{1,0:T(8,128)(2,1)S(1)}, bf16[128,1024]{1,0:T(8,128)(2,1)S(1)}, u32[]{:S(2)}, u32[]{:S(2)}) %collective-permute-start.1) | collective-permute-done | bytes 262176 | tf_op jit(solution)/shard_map/ppermute | solution.py:482
  35.5 6.1 %collective-permute-start.5 = (bf16[128,1024]{1,0:T(8,128)(2,1)S(1)}, bf16[128,1024]{1,0:T(8,128)(2,1)S(1)}, u32[]{:S(2)}, u32[]{:S(2)}) collective-permute-start(bf16[128,1024]{1,0:T(8,128)(2,1)S(1)} %convert_element_type.176), channel_id=1, source_target_pairs={{0,1},{1,2},{2,3},{3,0},{4,5},{5,6},{6,7},{7,4},{8,9},{9,10},{10,1... | collective-permute-start | bytes 786440 | tf_op jit(solution)/shard_map/ppermute | solution.py:482
  43.9 6.0 %collective-permute-done.5 = bf16[128,1024]{1,0:T(8,128)(2,1)S(1)} collective-permute-done((bf16[128,1024]{1,0:T(8,128)(2,1)S(1)}, bf16[128,1024]{1,0:T(8,128)(2,1)S(1)}, u32[]{:S(2)}, u32[]{:S(2)}) %collective-permute-start.5) | collective-permute-done | bytes 262176 | tf_op jit(solution)/shard_map/ppermute | solution.py:482
  49.9 8.9 %collective-permute-done.6 = bf16[128,1024]{1,0:T(8,128)(2,1)S(1)} collective-permute-done((bf16[128,1024]{1,0:T(8,128)(2,1)S(1)}, bf16[128,1024]{1,0:T(8,128)(2,1)S(1)}, u32[]{:S(2)}, u32[]{:S(2)}) %collective-permute-start.6) | collective-permute-done | bytes 262176 | tf_op jit(solution)/shard_map/ppermute | solution.py:482
  61.5 12.3 %collective-permute-done.8.refs_5_.refs_7_ = bf16[2,128,1024]{2,1,0:T(8,128)(2,1)S(1)} collective-permute-done((bf16[2,128,1024]{2,1,0:T(8,128)(2,1)S(1)}, bf16[2,128,1024]{2,1,0:T(8,128)(2,1)S(1)}, u32[]{:S(2)}, u32[]{:S(2)}) %collective-permute-start.8) | collective-permute-done | bytes 524320 | tf_op jit(solution)/shard_map/ppermute | solution.py:478
  76.8 6.1 %collective-permute-start.17 = (f32[1536]{0:T(1024)S(1)}, f32[1536]{0:T(1024)S(1)}, u32[]{:S(2)}, u32[]{:S(2)}) collective-permute-start(f32[1536]{0:T(1024)S(1)} %pad_maximum_fusion.19), channel_id=1, source_target_pairs={{0,1},{1,2},{2,3},{3,0},{4,5},{5,6},{6,7},{7,4},{8,9},{9,10},{10,1... | collective-permute-start | bytes 18440 | tf_op jit(solution)/shard_map/ppermute | solution.py:482
  94.8 4.3 %collective-permute-start.21 = (bf16[128,1024]{1,0:T(8,128)(2,1)S(1)}, bf16[128,1024]{1,0:T(8,128)(2,1)}, u32[]{:S(2)}, u32[]{:S(2)}) collective-permute-start(bf16[128,1024]{1,0:T(8,128)(2,1)S(1)} %convert_bitcast_fusion), channel_id=1, source_target_pairs={{0,2},{1,3},{2,0},{3,1},{4,6},{5,7},{6,4},{7,5},{8,10},{9,11},{10,... | collective-permute-start | bytes 786440 | tf_op jit(solution)/shard_map/ppermute | solution.py:482
  100.1 18.9 %shard_map.467 = (bf16[4,577,768]{2,1,0:T(8,128)(2,1)}, bf16[4,577,256]{2,1,0:T(8,128)(2,1)}, f32[4,8,577]{2,1,0:T(8,128)}) custom-call(bf16[577,1024]{1,0:T(8,128)(2,1)} %get-tuple-element.327.refs_0_.refs_3_.x, f32[4,1,768]{2,1,0:T(1,128)} %copy.56.refs_1_, bf16[4,128,1024]{2,1,0:T(8,128)(2,1)} %copy-done, bf16[4,128,1024]{2,1,0:T(8,128)(2,1)} %copy-done.1, ...), custom_call_target="tpu_custom_call" | custom-call | tf_op jit(solution)/shard_map/pallas_call | solution.py:130
  122.6 7.7 %shard_map.468 = (f32[577,1024]{1,0:T(8,128)}, bf16[577,1024]{1,0:T(8,128)(2,1)}) custom-call(bf16[4,577,256]{2,1,0:T(8,128)(2,1)} %get-tuple-element.325.refs_0_.inner, f32[577,1024]{1,0:T(8,128)} %get-tuple-element.258.refs_1_, f32[2,1024]{1,0:T(2,128)} %get-tuple-element.259.refs_2_.refs_5_.refs_3_, f32[4,1024]{1,0:T(4,128)} %get-tuple-element.260.refs_3_.refs_6_, ...), custom_call_target="tpu_custom_call" | custom-call | tf_op jit(solution)/shard_map/pallas_call | solution.py:130
  142.1 14.7 %shard_map.469 = (bf16[4,577,1024]{2,1,0:T(8,128)(2,1)}, bf16[4,577,1024]{2,1,0:T(8,128)(2,1)}, bf16[4,512,1024]{2,1,0:T(8,128)(2,1)}) custom-call(bf16[577,1024]{1,0:T(8,128)(2,1)} %get-tuple-element.263.refs_0_.refs_7_.x, f32[4,1,1024]{2,1,0:T(1,128)} %broadcast_in_dim.13.refs_1_, bf16[577,1024]{1,0:T(8,128)(2,1)} %get-tuple-element.284.refs_2_.x.refs_0_, ...), custom_call_target="tpu_custom_call" | custom-call | tf_op jit(solution)/shard_map/pallas_call | solution.py:130
  165.3 6.4 %collective-permute-done.34.other = bf16[4,512,1024]{2,1,0:T(8,128)(2,1)S(1)} collective-permute-done((bf16[4,512,1024]{2,1,0:T(8,128)(2,1)}, bf16[4,512,1024]{2,1,0:T(8,128)(2,1)S(1)}, u32[]{:S(2)}, u32[]{:S(2)}) %collective-permute-start.34) | collective-permute-done | bytes 4194336 | tf_op jit(solution)/shard_map/ppermute | solution.py:478
  173.6 8.0 %shard_map.470 = (bf16[4,128,1024]{2,1,0:T(8,128)(2,1)}, bf16[4,128,1024]{2,1,0:T(8,128)(2,1)}, bf16[4,128,1024]{2,1,0:T(8,128)(2,1)}, bf16[2,128,1024]{2,1,0:T(8,128)(2,1)}, bf16[2,128,1024]{2,1,0:T(8,128)(2,1)}) custom-call(bf16[577,1024]{1,0:T(8,128)(2,1)} %get-tuple-element.284.refs_2_.x.refs_0_, bf16[4,577,1024]{2,1,0:T(8,128)(2,1)} %get-tuple-element.275.inner.refs_2_, ...), custom_call_target="tpu_custom_call" | custom-call | tf_op jit(solution)/shard_map/pallas_call | solution.py:130
  185.4 31.5 %shard_map.471 = (bf16[4,577,1024]{2,1,0:T(8,128)(2,1)}, f32[4,1,1024]{2,1,0:T(1,128)}, bf16[4,512,1024]{2,1,0:T(8,128)(2,1)}, f32[577,1024]{1,0:T(8,128)}, f32[...) custom-call(s32[8]{0:T(128)} %broadcast_xor_fusion.order, ...), custom_call_target="tpu_custom_call" | custom-call | tf_op jit(solution)/shard_map/pallas_call | solution.py:130
  227.3 8.0 %shard_map.472 = (bf16[4,128,1024]{2,1,0:T(8,128)(2,1)}, bf16[4,128,1024]{2,1,0:T(8,128)(2,1)}, bf16[4,128,1024]{2,1,0:T(8,128)(2,1)}, bf16[2,128,1024]{2,1,0:T(8,128)(2,1)}, bf16[2,128,1024]{2,1,0:T(8,128)(2,1)}) custom-call(bf16[577,1024]{1,0:T(8,128)(2,1)} %get-tuple-element.263.refs_0_.refs_7_.x, bf16[4,577,1024]{2,1,0:T(8,128)(2,1)} %get-tuple-element.300.inner, ...), custom_call_target="tpu_custom_call" | custom-call | tf_op jit(solution)/shard_map/pallas_call | solution.py:130
  237.2 29.7 %shard_map.473 = (bf16[4,577,768]{2,1,0:T(8,128)(2,1)}, f32[4,2,256]{2,1,0:T(2,128)}, bf16[4,512,768]{2,1,0:T(8,128)(2,1)}) custom-call(bf16[577,1024]{1,0:T(8,128)(2,1)} %get-tuple-element.315.refs_0_.x, bf16[4,577,768]{2,1,0:T(8,128)(2,1)} %get-tuple-element.316.refs_1_, f32[4,8,577]{2,1,0:T(8,128)} %get-tuple-element.317.refs_2_, ...), custom_call_target="tpu_custom_call" | custom-call | tf_op jit(solution)/shard_map/pallas_call | solution.py:130
  280.4 4.7 %shard_map.474 = bf16[4,512,256]{2,1,0:T(8,128)(2,1)} custom-call(bf16[577,1024]{1,0:T(8,128)(2,1)} %get-tuple-element.315.refs_0_.x, bf16[4,577,256]{2,1,0:T(8,128)(2,1)} %get-tuple-element.325.refs_0_.inner), custom_call_target="tpu_custom_call" | custom-call | tf_op jit(solution)/shard_map/pallas_call | solution.py:130
  289.6 6.9 %shard_map.475 = (bf16[4,128,768]{2,1,0:T(8,128)(2,1)}, bf16[4,128,768]{2,1,0:T(8,128)(2,1)}, bf16[4,128,768]{2,1,0:T(8,128)(2,1)}, bf16[2,128,768]{2,1,0:T(8,128)(2,1)}, bf16[2,128,768]{2,1,0:T(8,128)(2,1)}) custom-call(bf16[577,1024]{1,0:T(8,128)(2,1)} %get-tuple-element.327.refs_0_.refs_3_.x, bf16[4,577,768]{2,1,0:T(8,128)(2,1)} %get-tuple-element.336.inner.refs_0_, ...), custom_call_target="tpu_custom_call" | custom-call | tf_op jit(solution)/shard_map/pallas_call | solution.py:130
  301.1 5.4 %reduce-scatter.4.cloned.1.call-done = bf16[1,128,1024]{2,1,0:T(8,128)(2,1)} async-done(((bf16[4,128,1024]{2,1,0:T(8,128)(2,1)}), bf16[1,128,1024]{2,1,0:T(8,128)(2,1)}) %reduce-scatter.4.cloned.1.call-update) | async-done | bytes 262160 | tf_op jit(solution)/shard_map/reduce_scatter | solution.py:530
  307.6 13.0 %shard_map.476 = (f32[577,1024]{1,0:T(8,128)}, f32[2,1024]{1,0:T(2,128)}) custom-call(s32[8]{0:T(128)} %broadcast_xor_fusion.order, bf16[4,577,768]{2,1,0:T(8,128)(2,1)} %get-tuple-element.336.inner.refs_0_, f32[577,1024]{1,0:T(8,128)} %get-tuple-element.258.refs_1_, f32[577,1024]{1,0:T(8,128)} %get-tuple-element.337.refs_2_, ...), custom_call_target="tpu_custom_call" | custom-call | tf_op jit(solution)/shard_map/pallas_call | solution.py:130
  323.6 4.6 %shard_map.477 = (bf16[4,128,256]{2,1,0:T(8,128)(2,1)}, bf16[4,128,256]{2,1,0:T(8,128)(2,1)}, bf16[4,128,256]{2,1,0:T(8,128)(2,1)}, bf16[2,128,256]{2,1,0:T(8,128)(2,1)}, bf16[2,128,256]{2,1,0:T(8,128)(2,1)}) custom-call(bf16[577,1024]{1,0:T(8,128)(2,1)} %get-tuple-element.315.refs_0_.x, bf16[4,577,256]{2,1,0:T(8,128)(2,1)} %get-tuple-element.325.refs_0_.inner, ...), custom_call_target="tpu_custom_call" | custom-call | tf_op jit(solution)/shard_map/pallas_call | solution.py:130
  352.7 8.7 %collective-permute-done.61 = f32[12,1024]{1,0:T(8,128)S(1)} collective-permute-done((f32[12,1024]{1,0:T(8,128)S(1)}, f32[12,1024]{1,0:T(8,128)S(1)}, u32[]{:S(2)}, u32[]{:S(2)}) %collective-permute-start.61) | collective-permute-done | bytes 49184 | tf_op jit(solution)/shard_map/ppermute | solution.py:486
  385.6 6.1 %collective-permute-done.64 = bf16[128,768]{1,0:T(8,128)(2,1)S(1)} collective-permute-done((bf16[128,768]{1,0:T(8,128)(2,1)S(1)}, bf16[128,768]{1,0:T(8,128)(2,1)S(1)}, u32[]{:S(2)}, u32[]{:S(2)}) %collective-permute-start.64) | collective-permute-done | bytes 196640 | tf_op jit(solution)/shard_map/ppermute | solution.py:482
  391.7 8.9 %collective-permute-done.65 = bf16[128,768]{1,0:T(8,128)(2,1)S(1)} collective-permute-done((bf16[128,768]{1,0:T(8,128)(2,1)S(1)}, bf16[128,768]{1,0:T(8,128)(2,1)S(1)}, u32[]{:S(2)}, u32[]{:S(2)}) %collective-permute-start.65) | collective-permute-done | bytes 196640 | tf_op jit(solution)/shard_map/ppermute | solution.py:482
  (413 shorter events, 149.6 us)
Async XLA Ops:
  7.2 299.3 %reduce-scatter.4.cloned.1.call-start = ((), (), s32[]{:S(2)}) async-start(), calls=%async_computation.3 | async-start | bytes 1310720 | tf_op jit(solution)/shard_map/reduce_scatter | solution.py:530
  32.4 26.4 %collective-permute-start.3 = (bf16[4,128,1024]{2,1,0:T(8,128)(2,1)S(1)}, bf16[4,128,1024]{2,1,0:T(8,128)(2,1)S(1)}, u32[]{:S(2)}, u32[]{:S(2)}) collective-permute-start(bf16[4,128,1024]{2,1,0:T(8,128)(2,1)S(1)} %pad_maximum_fusion.refs_2_.refs_4_), channel_id=1, source_target_pairs={{0,8},{4,12},{8,0},{12,4},{16,24},{20,28},{24,16},{28,20},{1,9},{5... | collective-permute-start | bytes 3145736 | tf_op jit(solution)/shard_map/ppermute | solution.py:478
  33.9 24.9 %collective-permute-start.4 = (bf16[4,128,1024]{2,1,0:T(8,128)(2,1)S(1)}, bf16[4,128,1024]{2,1,0:T(8,128)(2,1)S(1)}, u32[]{:S(2)}, u32[]{:S(2)}) collective-permute-start(bf16[4,128,1024]{2,1,0:T(8,128)(2,1)S(1)} %pad_maximum_fusion.refs_2_.refs_4_), channel_id=1, source_target_pairs={{0,16},{4,20},{8,24},{12,28},{16,0},{20,4},{24,8},{28,12},{1,17},{... | collective-permute-start | bytes 3145736 | tf_op jit(solution)/shard_map/ppermute | solution.py:478
  74.9 44.1 %collective-permute-start.13 = (bf16[4,128,1024]{2,1,0:T(8,128)(2,1)S(1)}, bf16[4,128,1024]{2,1,0:T(8,128)(2,1)S(1)}, u32[]{:S(2)}, u32[]{:S(2)}) collective-permute-start(bf16[4,128,1024]{2,1,0:T(8,128)(2,1)S(1)} %pad_maximum_fusion.1.refs_3_.refs_18_), channel_id=1, source_target_pairs={{0,8},{4,12},{8,0},{12,4},{16,24},{20,28},{24,16},{28,20},{1,9},{5... | collective-permute-start | bytes 3145736 | tf_op jit(solution)/shard_map/ppermute | solution.py:478
  75.5 43.5 %collective-permute-start.14 = (bf16[4,128,1024]{2,1,0:T(8,128)(2,1)S(1)}, bf16[4,128,1024]{2,1,0:T(8,128)(2,1)S(1)}, u32[]{:S(2)}, u32[]{:S(2)}) collective-permute-start(bf16[4,128,1024]{2,1,0:T(8,128)(2,1)S(1)} %pad_maximum_fusion.1.refs_3_.refs_18_), channel_id=1, source_target_pairs={{0,16},{4,20},{8,24},{12,28},{16,0},{20,4},{24,8},{28,12},{1,17},{... | collective-permute-start | bytes 3145736 | tf_op jit(solution)/shard_map/ppermute | solution.py:478
  94.5 24.4 %collective-permute-start.20 = (bf16[128,1024]{1,0:T(8,128)(2,1)S(1)}, bf16[128,1024]{1,0:T(8,128)(2,1)}, u32[]{:S(2)}, u32[]{:S(2)}) collective-permute-start(bf16[128,1024]{1,0:T(8,128)(2,1)S(1)} %convert_bitcast_fusion), channel_id=1, source_target_pairs={{0,1},{1,2},{2,3},{3,0},{4,5},{5,6},{6,7},{7,4},{8,9},{9,10},{10,1... | collective-permute-start | bytes 786440 | tf_op jit(solution)/shard_map/ppermute | solution.py:482
  94.8 24.2 %collective-permute-start.21 = (bf16[128,1024]{1,0:T(8,128)(2,1)S(1)}, bf16[128,1024]{1,0:T(8,128)(2,1)}, u32[]{:S(2)}, u32[]{:S(2)}) collective-permute-start(bf16[128,1024]{1,0:T(8,128)(2,1)S(1)} %convert_bitcast_fusion), channel_id=1, source_target_pairs={{0,2},{1,3},{2,0},{3,1},{4,6},{5,7},{6,4},{7,5},{8,10},{9,11},{10,... | collective-permute-start | bytes 786440 | tf_op jit(solution)/shard_map/ppermute | solution.py:482
  135.3 24.8 %collective-permute-start.28 = (bf16[4,128,1024]{2,1,0:T(8,128)(2,1)S(1)}, bf16[4,128,1024]{2,1,0:T(8,128)(2,1)S(1)}, u32[]{:S(2)}, u32[]{:S(2)}) collective-permute-start(bf16[4,128,1024]{2,1,0:T(8,128)(2,1)S(1)} %pad_maximum_fusion.2.refs_8_), channel_id=1, source_target_pairs={{0,8},{4,12},{8,0},{12,4},{16,24},{20,28},{24,16},{28,20},{1,9},{5... | collective-permute-start | bytes 3145736 | tf_op jit(solution)/shard_map/ppermute | solution.py:478
  136.8 24.4 %collective-permute-start.29 = (bf16[4,128,1024]{2,1,0:T(8,128)(2,1)S(1)}, bf16[4,128,1024]{2,1,0:T(8,128)(2,1)S(1)}, u32[]{:S(2)}, u32[]{:S(2)}) collective-permute-start(bf16[4,128,1024]{2,1,0:T(8,128)(2,1)S(1)} %pad_maximum_fusion.2.refs_8_), channel_id=1, source_target_pairs={{0,16},{4,20},{8,24},{12,28},{16,0},{20,4},{24,8},{28,12},{1,17},{... | collective-permute-start | bytes 3145736 | tf_op jit(solution)/shard_map/ppermute | solution.py:478
  182.3 34.6 %collective-permute-start.40 = (bf16[2,128,1024]{2,1,0:T(8,128)(2,1)}, bf16[2,128,1024]{2,1,0:T(8,128)(2,1)S(1)}, u32[]{:S(2)}, u32[]{:S(2)}) collective-permute-start(bf16[2,128,1024]{2,1,0:T(8,128)(2,1)} %get-tuple-element.293), channel_id=1, source_target_pairs={{0,16},{4,20},{8,24},{12,28},{16,0},{20,4},{24,8},{28,12},{1,17},{... | collective-permute-start | bytes 1572872 | tf_op jit(solution)/shard_map/ppermute | solution.py:478
  183.5 33.5 %collective-permute-start.41 = (bf16[2,128,1024]{2,1,0:T(8,128)(2,1)}, bf16[2,128,1024]{2,1,0:T(8,128)(2,1)S(1)}, u32[]{:S(2)}, u32[]{:S(2)}) collective-permute-start(bf16[2,128,1024]{2,1,0:T(8,128)(2,1)} %get-tuple-element.294), channel_id=1, source_target_pairs={{0,8},{4,12},{8,0},{12,4},{16,24},{20,28},{24,16},{28,20},{1,9},{5... | collective-permute-start | bytes 1572872 | tf_op jit(solution)/shard_map/ppermute | solution.py:478
  219.5 47.4 %collective-permute-start.46 = (bf16[4,128,1024]{2,1,0:T(8,128)(2,1)S(1)}, bf16[4,128,1024]{2,1,0:T(8,128)(2,1)}, u32[]{:S(2)}, u32[]{:S(2)}) collective-permute-start(bf16[4,128,1024]{2,1,0:T(8,128)(2,1)S(1)} %pad_maximum_fusion.4), channel_id=1, source_target_pairs={{0,16},{4,20},{8,24},{12,28},{16,0},{20,4},{24,8},{28,12},{1,17},{... | collective-permute-start | bytes 3145736 | tf_op jit(solution)/shard_map/ppermute | solution.py:478
  221.2 45.7 %collective-permute-start.45 = (bf16[4,128,1024]{2,1,0:T(8,128)(2,1)S(1)}, bf16[4,128,1024]{2,1,0:T(8,128)(2,1)S(1)}, u32[]{:S(2)}, u32[]{:S(2)}) collective-permute-start(bf16[4,128,1024]{2,1,0:T(8,128)(2,1)S(1)} %pad_maximum_fusion.3), channel_id=1, source_target_pairs={{0,8},{4,12},{8,0},{12,4},{16,24},{20,28},{24,16},{28,20},{1,9},{5... | collective-permute-start | bytes 3145736 | tf_op jit(solution)/shard_map/ppermute | solution.py:478
  235.3 31.6 %collective-permute-start.43 = (bf16[2,128,1024]{2,1,0:T(8,128)(2,1)}, bf16[2,128,1024]{2,1,0:T(8,128)(2,1)S(1)}, u32[]{:S(2)}, u32[]{:S(2)}) collective-permute-start(bf16[2,128,1024]{2,1,0:T(8,128)(2,1)} %get-tuple-element.309), channel_id=1, source_target_pairs={{0,16},{4,20},{8,24},{12,28},{16,0},{20,4},{24,8},{28,12},{1,17},{... | collective-permute-start | bytes 1572872 | tf_op jit(solution)/shard_map/ppermute | solution.py:478
  236.5 30.4 %collective-permute-start.44 = (bf16[2,128,1024]{2,1,0:T(8,128)(2,1)}, bf16[2,128,1024]{2,1,0:T(8,128)(2,1)S(1)}, u32[]{:S(2)}, u32[]{:S(2)}) collective-permute-start(bf16[2,128,1024]{2,1,0:T(8,128)(2,1)} %get-tuple-element.310), channel_id=1, source_target_pairs={{0,8},{4,12},{8,0},{12,4},{16,24},{20,28},{24,16},{28,20},{1,9},{5... | collective-permute-start | bytes 1572872 | tf_op jit(solution)/shard_map/ppermute | solution.py:478
  280.3 93.0 %reduce-scatter.6.cloned.1.call-start = ((), (), s32[]{:S(2)}) async-start(), calls=%async_computation.4 | async-start | bytes 1310720 | tf_op jit(solution)/shard_map/reduce_scatter | solution.py:530
  286.4 41.8 %collective-permute-start.51 = (bf16[4,128,1024]{2,1,0:T(8,128)(2,1)}, bf16[4,128,1024]{2,1,0:T(8,128)(2,1)}, u32[]{:S(2)}, u32[]{:S(2)}) collective-permute-start(bf16[4,128,1024]{2,1,0:T(8,128)(2,1)} %pad_maximum_fusion.6), channel_id=1, source_target_pairs={{0,16},{4,20},{8,24},{12,28},{16,0},{20,4},{24,8},{28,12},{1,17},{... | collective-permute-start | bytes 3145736 | tf_op jit(solution)/shard_map/ppermute | solution.py:478
  296.5 26.2 %collective-permute-start.52 = (bf16[4,512,256]{2,1,0:T(8,128)(2,1)}, bf16[4,512,256]{2,1,0:T(8,128)(2,1)S(1)}, u32[]{:S(2)}, u32[]{:S(2)}) collective-permute-start(bf16[4,512,256]{2,1,0:T(8,128)(2,1)} %shard_map.474), channel_id=1, source_target_pairs={{0,4},{4,0},{8,12},{12,8},{16,20},{20,16},{24,28},{28,24},{1,5},{5... | collective-permute-start | bytes 3145736 | tf_op jit(solution)/shard_map/ppermute | solution.py:478
  296.9 31.3 %collective-permute-start.50 = (bf16[4,128,1024]{2,1,0:T(8,128)(2,1)S(1)}, bf16[4,128,1024]{2,1,0:T(8,128)(2,1)}, u32[]{:S(2)}, u32[]{:S(2)}) collective-permute-start(bf16[4,128,1024]{2,1,0:T(8,128)(2,1)S(1)} %pad_maximum_fusion.5), channel_id=1, source_target_pairs={{0,8},{4,12},{8,0},{12,4},{16,24},{20,28},{24,16},{28,20},{1,9},{5... | collective-permute-start | bytes 3145736 | tf_op jit(solution)/shard_map/ppermute | solution.py:478
  299.1 29.1 %collective-permute-start.48 = (bf16[2,128,768]{2,1,0:T(8,128)(2,1)}, bf16[2,128,768]{2,1,0:T(8,128)(2,1)S(1)}, u32[]{:S(2)}, u32[]{:S(2)}) collective-permute-start(bf16[2,128,768]{2,1,0:T(8,128)(2,1)} %get-tuple-element.339), channel_id=1, source_target_pairs={{0,16},{4,20},{8,24},{12,28},{16,0},{20,4},{24,8},{28,12},{1,17},{... | collective-permute-start | bytes 1179656 | tf_op jit(solution)/shard_map/ppermute | solution.py:478
  300.4 30.4 %collective-permute-start.49 = (bf16[2,128,768]{2,1,0:T(8,128)(2,1)}, bf16[2,128,768]{2,1,0:T(8,128)(2,1)}, u32[]{:S(2)}, u32[]{:S(2)}) collective-permute-start(bf16[2,128,768]{2,1,0:T(8,128)(2,1)} %get-tuple-element.340), channel_id=1, source_target_pairs={{0,8},{4,12},{8,0},{12,4},{16,24},{20,28},{24,16},{28,20},{1,9},{5... | collective-permute-start | bytes 1179656 | tf_op jit(solution)/shard_map/ppermute | solution.py:478
  334.2 67.7 %reduce-scatter.8.cloned.1.call-start = ((), (), s32[]{:S(2)}) async-start(), calls=%async_computation.5 | async-start | bytes 327680 | tf_op jit(solution)/shard_map/reduce_scatter | solution.py:530
  342.4 31.9 %collective-permute-start.54 = (bf16[4,128,768]{2,1,0:T(8,128)(2,1)}, bf16[4,128,768]{2,1,0:T(8,128)(2,1)}, u32[]{:S(2)}, u32[]{:S(2)}) collective-permute-start(bf16[4,128,768]{2,1,0:T(8,128)(2,1)} %pad_maximum_fusion.10), channel_id=1, source_target_pairs={{0,16},{4,20},{8,24},{12,28},{16,0},{20,4},{24,8},{28,12},{1,17},{... | collective-permute-start | bytes 2359304 | tf_op jit(solution)/shard_map/ppermute | solution.py:478
  346.4 27.9 %collective-permute-start.53 = (bf16[4,128,768]{2,1,0:T(8,128)(2,1)}, bf16[4,128,768]{2,1,0:T(8,128)(2,1)}, u32[]{:S(2)}, u32[]{:S(2)}) collective-permute-start(bf16[4,128,768]{2,1,0:T(8,128)(2,1)} %pad_maximum_fusion.9), channel_id=1, source_target_pairs={{0,8},{4,12},{8,0},{12,4},{16,24},{20,28},{24,16},{28,20},{1,9},{5... | collective-permute-start | bytes 2359304 | tf_op jit(solution)/shard_map/ppermute | solution.py:478
  (133 other events, 1405.8 us)
Sparse Core Ops, SparseCore 0:
  280.4 26.0 reduce-scatter.3
  334.4 28.7 reduce-scatter.5
  378.3 23.1 reduce-scatter.7
where the time goes:
time: 418 us; the launch traced here: 413 us
  Pallas kernels  155 us (37%)
  waiting for transfers between devices  103 us (25%)
  starting transfers between devices  68.8 us (16%)
  other arithmetic  31.7 us (8%)
  local copies, waits for them, and re-layouts  30.8 us (7%)
  between operations  23.4 us (6%)
    pallas_call x11, Pallas kernels, grouped(): pl.pallas_call(kernel, grid_spec=pltpu.PrefetchScalarGridSpec(num_scalar_...  148 us
    ppermute x15, waiting for transfers between devices, turn(): lax.ppermute(values, 'narrow', [(at, (at + step) % 4) for at in range(4)])  45 us
    ppermute x50, waiting for transfers between devices, swap(): return lax.ppermute(values, 'wide', [(at, at ^ bit) for at in range(8)])  40.6 us
    ppermute x50, starting transfers between devices, swap(): return lax.ppermute(values, 'wide', [(at, at ^ bit) for at in range(8)])  35.8 us
    ppermute x15, starting transfers between devices, turn(): lax.ppermute(values, 'narrow', [(at, (at + step) % 4) for at in range(4)])  30.7 us
    unnamed x188, local copies, waits for them, and re-layouts  18.8 us
    ppermute x2, waiting for transfers between devices, cross(): return lax.ppermute(values, 'narrow', [(at, at ^ bit) for at in range(4)])  12.3 us
  transfers between devices with their start and end apart: 70, of which 23 were waited for; matrix products, arithmetic and copies ran while one was open for 9% of the time, Pallas kernels for 37%

commit v1 on v0

--- a/solution.py
+++ b/solution.py
@@ -472,6 +472,22 @@
         scratch=[pltpu.VMEM((rows, D), full)],
         prefetch=1,
     )
+
+
+def turned_adam_kernel(rate, grad, weight, first, second, grad_out, second_out, weight_out):
+    turned = grad[...].T
+    grad_out[...] = turned
+    second_new, updated = adam_step(weight[...], turned, first[...], second[...], rate, decay_rate)
+    second_out[...] = second_new
+    weight_out[...] = updated
+
+
+def turned_adam(rate, grad, weight, first, second):
+    return pl.pallas_call(
+        functools.partial(turned_adam_kernel, rate),
+        out_shape=[struct(weight.shape, full)] * 3,
+        compiler_params=big,
+    )(grad, weight, first, second)
 
 
 def swap(values, bit):
@@ -576,15 +592,16 @@
     at_narrow = lax.axis_index("narrow")
     if tuned:
         order = jnp.bitwise_xor(place, jnp.array([0, 2, 4, 6, 1, 3, 5, 7], jnp.int32)).astype(jnp.int32)
-        group_order = (at_narrow - jnp.arange(narrow)) % narrow
+        steps = [lax.rem(at_narrow + (narrow - at), narrow) for at in range(narrow)]
     else:
         order = jnp.arange(BLOCKS, dtype=jnp.int32)
-        group_order = jnp.arange(narrow)
+        steps = list(range(narrow))
 
     triple_block = jnp.concatenate([triple_weight[:, at].astype(low) for at in range(3)] + [output_weight.astype(low).T], axis=1)
     expand_block = expand_weight.astype(low)
     shrink_block = shrink_weight.astype(low).T
-    bias_block = jnp.concatenate([head_biases[0], head_biases[1], expand_biases])
+    zeros = jnp.zeros((local,), full)
+    bias_rows = jnp.stack([jnp.concatenate([head_biases[0], zeros, head_biases[1], zeros]), expand_biases])
 
     def begin(order, tokens, cotangent):
         return pl.pallas_call(
@@ -603,37 +620,42 @@
         )(order, tokens, cotangent, norm_gains, shift_biases)
 
     def split_bias(biases):
-        triple_bias = jnp.concatenate(
-            [biases[:, :local], jnp.zeros((narrow, local), full), biases[:, local : 2 * local]], axis=1
-        )
-        return triple_bias[:, None], biases[:, 2 * local :][:, None]
+        return biases[:, 0:1, : 3 * local], biases[:, 1:2]
 
     if tuned:
-        triple_turns = around(triple_block)
+        high = lax.reduce_precision(bias_rows, 8, 7)
+        rest = bias_rows - high
+        mid = lax.reduce_precision(rest, 8, 7)
+        parts = jnp.concatenate([high, mid, rest - mid, jnp.zeros((10, hidden), full)]).astype(low)
+        ridden = jnp.concatenate([triple_block, parts], axis=0)
+        triple_turns = around(ridden)
         begun = begin(order, tokens, cotangent)
-        triple_turns, begun, triple_block, expand_block, shrink_block, bias_block = fence(
-            triple_turns, begun, triple_block, expand_block, shrink_block, bias_block
+        triple_turns, begun, ridden, expand_block, shrink_block = fence(
+            triple_turns, begun, ridden, expand_block, shrink_block
         )
         tok, normed, cot, cot_low, gains, shifts, cot_sum = begun
-        t_near = jnp.stack([triple_block, *triple_turns])
+        depth = triple_block.shape[0]
+        arrived = [ridden, *triple_turns]
+        t_near = jnp.stack([block[:depth] for block in arrived])
+        biases = jnp.stack([block[depth:] for block in arrived])
         t_x, t_y = swap(t_near, 2), swap(t_near, 4)
         expand_turns = around(expand_block)
-        t_near, t_x, t_y, expand_turns, expand_block, normed, bias_block = fence(
-            t_near, t_x, t_y, expand_turns, expand_block, normed, bias_block
+        t_near, t_x, t_y, expand_turns, expand_block, normed, biases = fence(
+            t_near, t_x, t_y, expand_turns, expand_block, normed, biases
         )
         t_f, t_g = swap(t_x[:2], 4), swap(t_y[2:], 2)
         t_near_c, t_x_c, t_y_c = swap(t_near, 1), swap(t_x, 1), swap(t_y, 1)
         e_near = jnp.stack([expand_block, *expand_turns])
-        t_f, t_g, t_near_c, t_x_c, t_y_c, e_near, normed, bias_block, shrink_block = fence(
-            t_f, t_g, t_near_c, t_x_c, t_y_c, e_near, normed, bias_block, shrink_block
+        biases = biases.astype(full)
+        triple_bias, widen_bias = split_bias(biases[:, 0:2] + biases[:, 2:4] + biases[:, 4:6])
+        t_f, t_g, t_near_c, t_x_c, t_y_c, e_near, normed, triple_bias, shrink_block = fence(
+            t_f, t_g, t_near_c, t_x_c, t_y_c, e_near, normed, triple_bias, shrink_block
         )
         e_x, e_y = swap(e_near, 2), swap(e_near, 4)
         t_f_c, t_g_c = swap(t_f, 1), swap(t_g, 1)
         triple_own = (t_near, t_x, t_y, t_f, t_g)
         triple_twin = (t_near_c, t_x_c, t_y_c, t_f_c, t_g_c)
-        bias_turns = around(bias_block)
-        triple_twin, bias_turns, normed, shrink_block = fence(triple_twin, bias_turns, normed, shrink_block)
-        triple_bias, widen_bias = split_bias(jnp.stack([bias_block, *bias_turns]))
+        triple_twin, normed, shrink_block = fence(triple_twin, normed, shrink_block)
         shrink_turns = around(shrink_block)
         packed, mixed, logs = attend(normed, triple_bias, triple_own, triple_twin)
         e_near, e_x, e_y, mixed, shrink_turns, shrink_block, tok = fence(
@@ -651,7 +673,7 @@
         expand_twin = (e_near_c, e_x_c, e_y_c, swap(e_f, 1), swap(e_g, 1))
     else:
         tok, normed, cot, cot_low, gains, shifts, cot_sum = begin(order, tokens, cotangent)
-        triple_bias, widen_bias = split_bias(lax.all_gather(bias_block, "narrow", axis=0, tiled=False))
+        triple_bias, widen_bias = split_bias(lax.all_gather(bias_rows, "narrow", axis=0, tiled=False))
         triple_own, triple_twin = plain_gather(triple_block)
         expand_own, expand_twin = plain_gather(expand_block)
         shrink_own, shrink_twin = plain_gather(shrink_block)
@@ -695,34 +717,39 @@
         s_over_x, s_over_y = swap(to_x, 2), swap(to_y, 4)
     else:
         e_other = jnp.zeros_like(e_twin)
+    o_twin = outer_twin(middle_low, mixed)
+    if tuned:
+        e_other, o_twin, expanded_low = fence(e_other, o_twin, expanded_low)
     e_pieces = outer_own(normed_two, expanded_low, e_other)
     if tuned:
-        e_pieces, middle_low, packed = fence(e_pieces, middle_low, packed)
+        e_pieces, middle_low, packed, o_twin = fence(e_pieces, middle_low, packed, o_twin)
         from_y, from_x = swap(e_pieces[3], 4), swap(e_pieces[4], 2)
+        o_other = swap(o_twin, 1)
+    else:
+        o_other = jnp.zeros_like(o_twin)
     triple_low, head_sums, t_twin = attend_back(middle_low, packed, logs, normed, triple_own, triple_twin, 3)
     if tuned:
-        from_y, from_x, s_over_x, s_over_y, t_twin, triple_low, e_pieces, s_pieces, mixed = fence(
-            from_y, from_x, s_over_x, s_over_y, t_twin, triple_low, e_pieces, s_pieces, mixed
+        from_y, from_x, s_over_x, s_over_y, t_twin, triple_low, e_pieces, s_pieces, mixed, o_other = fence(
+            from_y, from_x, s_over_x, s_over_y, t_twin, triple_low, e_pieces, s_pieces, mixed, o_other
         )
         t_other = swap(t_twin, 1)
         to_x, to_y = near_sends(e_pieces, from_y, from_x)
         e_over_x, e_over_y = swap(to_x, 2), swap(to_y, 4)
-        o_twin = outer_twin(middle_low, mixed)
-        t_other, o_twin, triple_low, normed = fence(t_other, o_twin, triple_low, normed)
+        shrink_grad = narrow_scatter(s_pieces[0], s_over_x, s_over_y, steps)
     else:
         t_other = jnp.zeros_like(t_twin)
-        o_twin = outer_twin(middle_low, mixed)
+    o_pieces = outer_own(middle_low, mixed, o_other)
+    if tuned:
+        t_other, o_pieces, triple_low, normed = fence(t_other, o_pieces, triple_low, normed)
     t_pieces = outer_own(normed, triple_low, t_other)
     if tuned:
-        t_pieces, o_twin, triple_low = fence(t_pieces, o_twin, triple_low)
+        t_pieces, triple_low = fence(t_pieces, triple_low)
         t_from_y, t_from_x = swap(t_pieces[3], 4), swap(t_pieces[4], 2)
-        o_other = swap(o_twin, 1)
-        shrink_grad = narrow_scatter(s_pieces[0], s_over_x, s_over_y, group_order)
-    else:
-        o_other = jnp.zeros_like(o_twin)
     input_gradient, one_sums = norm_one(
         order, triple_low, tok, middle_grad, gains, triple_own, triple_twin
     )
+    turned_heads = jnp.stack([lax.dynamic_index_in_dim(head_sums, step, 0, keepdims=False) for step in steps], axis=1)
+    turned_widen = jnp.concatenate([lax.dynamic_index_in_dim(widen_sum, step, 0, keepdims=False) for step in steps])
     small = jnp.concatenate(
         [
             one_sums[0:1],
@@ -730,33 +757,35 @@
             one_sums[1:2],
             two_sums[1:3],
             cot_sum,
-            head_sums[group_order].transpose(1, 0, 2).reshape(2, D),
-            widen_sum[group_order].reshape(-1, D),
+            turned_heads.reshape(2, D),
+            turned_widen.reshape(-1, D),
         ],
         axis=0,
     )
-    o_pieces = outer_own(middle_low, mixed, o_other)
     if tuned:
-        t_from_y, t_from_x, small, t_pieces, e_over_x, e_over_y, o_pieces, shrink_grad = fence(
-            t_from_y, t_from_x, small, t_pieces, e_over_x, e_over_y, o_pieces, shrink_grad
+        t_from_y, t_from_x, small, t_pieces, e_over_x, e_over_y, o_pieces = fence(
+            t_from_y, t_from_x, small, t_pieces, e_over_x, e_over_y, o_pieces
         )
         to_x, to_y = near_sends(t_pieces, t_from_y, t_from_x)
+        to_x, to_y, small, e_over_x, e_over_y, o_pieces = fence(to_x, to_y, small, e_over_x, e_over_y, o_pieces)
         t_over_x, t_over_y = swap(to_x, 2), swap(to_y, 4)
-        expand_gradient = narrow_scatter(e_pieces[0], e_over_x, e_over_y, group_order)
+        expand_gradient = narrow_scatter(e_pieces[0], e_over_x, e_over_y, steps)
         from_y, from_x = swap(o_pieces[3], 4), swap(o_pieces[4], 2)
         to_x, to_y = near_sends(o_pieces, from_y, from_x)
         o_over_x, o_over_y = swap(to_x, 2), swap(to_y, 4)
         small = small + swap(small, 1)
         small = small + cross(small, 1)
+        shrink_done = turned_adam(0.05, shrink_grad, shrink_weight, shrink_first, shrink_second)
+        t_over_x, t_over_y, o_over_x, o_over_y, small, expand_gradient, shrink_done = fence(
+            t_over_x, t_over_y, o_over_x, o_over_y, small, expand_gradient, shrink_done
+        )
+        t_last = last_sends(t_pieces[0], t_over_x, t_over_y)
+        t_last, small, expand_gradient, o_over_x, o_over_y = fence(t_last, small, expand_gradient, o_over_x, o_over_y)
         small = small + cross(small, 2)
         small = small + swap(small, 2)
         small = small + swap(small, 4)
-        t_over_x, t_over_y, o_over_x, o_over_y, small, expand_gradient = fence(
-            t_over_x, t_over_y, o_over_x, o_over_y, small, expand_gradient
-        )
-        t_last = last_sends(t_pieces[0], t_over_x, t_over_y)
         t_back = [turn(t_last[step], -step) for step in range(1, 4)]
-        output_grad = narrow_scatter(o_pieces[0], o_over_x, o_over_y, group_order)
+        output_grad = narrow_scatter(o_pieces[0], o_over_x, o_over_y, steps)
         triple_grad = last_sum(t_last[0], t_back)
     else:
         small = lax.psum(small, ("wide", "narrow"))
@@ -765,8 +794,9 @@
         expand_gradient = plain_scatter(e_pieces, e_twin)
         shrink_grad = plain_scatter(s_pieces, s_twin)
     triple_gradient = jnp.stack([triple_grad[:, at * local : (at + 1) * local] for at in range(3)], axis=1)
-    output_gradient = output_grad.T
-    shrink_gradient = shrink_grad.T
+    if not tuned:
+        shrink_done = turned_adam(0.05, shrink_grad, shrink_weight, shrink_first, shrink_second)
+    output_done = turned_adam(1.0, output_grad, output_weight, output_first, output_second)
     gains_gradient = small[0:2]
     shifts_gradient = small[2:6]
     heads_gradient = lax.dynamic_slice_in_dim(small[6:8], at_narrow * local, local, 1)
@@ -784,9 +814,9 @@
     )
     gradients = (
         triple_gradient,
-        output_gradient,
+        output_done[0],
         expand_gradient,
-        shrink_gradient,
+        shrink_done[0],
         gains_gradient,
         shifts_gradient,
         heads_gradient,
@@ -816,6 +846,9 @@
     decays = (decay_rate, decay_rate, decay_rate, decay_rate, 0.0, 0.0, 0.0, 0.0)
     results = [layer_output, input_gradient]
     for index in range(8):
+        if index in (1, 3):
+            results.extend(output_done if index == 1 else shrink_done)
+            continue
         renewed, updated = adam_step(
             params[index],
             gradients[index],

time: 418 us -> 388 us (0.928)
  waiting for transfers between devices: 103 us -> 84.4 us
  local copies, waits for them, and re-layouts: 30.8 us -> 22.6 us
  between operations: 23.4 us -> 15.4 us
  Pallas kernels: 155 us -> 160 us
    ppermute x2, waiting for transfers between devices: 12.3 us -> 1.39 us  [cross(): return lax.ppermute(values, 'narrow', [(at, at ^ bit) for at in range(4)])]
    ppermute x15 -> x12, waiting for transfers between devices: 45 us -> 35.3 us  [turn(): lax.ppermute(values, 'narrow', [(at, (at + step) % 4) for at in range(4)])]
    reduce_scatter x3, waiting for transfers between devices: 5.47 us -> 12.3 us  [narrow_scatter(): lax.psum_scatter(jnp.stack(parts), 'narrow', scatter_dimension=0, tiled=F...]
    unnamed x188 -> x162, local copies, waits for them, and re-layouts: 18.8 us -> 12.4 us
    ppermute x50, waiting for transfers between devices: 40.6 us -> 35.4 us  [swap(): return lax.ppermute(values, 'wide', [(at, at ^ bit) for at in range(8)])]
    pallas_call x0 -> x2, Pallas kernels: none -> 4.99 us  [turned_adam(): pl.pallas_call(functools.partial(turned_adam_kernel, rate), out_shape=[st...]
    ppermute x15 -> x12, starting transfers between devices: 30.7 us -> 30.1 us  [turn(): lax.ppermute(values, 'narrow', [(at, (at + step) % 4) for at in range(4)])]
  transfers between devices with their start and end apart: 70 -> 67, of which waited for: 23 -> 20; matrix products, arithmetic and copies ran while one was open for 9% -> 9% of each run, Pallas kernels for 37% -> 41%
where the time goes in v1:
time: 388 us; the launch traced here: 383 us
  Pallas kernels  160 us (41%)
  waiting for transfers between devices  84.4 us (22%)
  starting transfers between devices  71.3 us (18%)
  other arithmetic  29.2 us (8%)
  local copies, waits for them, and re-layouts  22.6 us (6%)
  between operations  15.4 us (4%)
    pallas_call x11, Pallas kernels, grouped(): pl.pallas_call(kernel, grid_spec=pltpu.PrefetchScalarGridSpec(num_scalar_...  148 us
    ppermute x50, waiting for transfers between devices, swap(): return lax.ppermute(values, 'wide', [(at, at ^ bit) for at in range(8)])  35.4 us
    ppermute x12, waiting for transfers between devices, turn(): lax.ppermute(values, 'narrow', [(at, (at + step) % 4) for at in range(4)])  35.3 us
    ppermute x50, starting transfers between devices, swap(): return lax.ppermute(values, 'wide', [(at, at ^ bit) for at in range(8)])  34.8 us
    ppermute x12, starting transfers between devices, turn(): lax.ppermute(values, 'narrow', [(at, (at + step) % 4) for at in range(4)])  30.1 us
    unnamed x162, local copies, waits for them, and re-layouts  12.4 us
    reduce_scatter x3, waiting for transfers between devices, narrow_scatter(): lax.psum_scatter(jnp.stack(parts), 'narrow', scatter_dimension=0, tiled=F...  12.3 us
  transfers between devices with their start and end apart: 67, of which 20 were waited for; matrix products, arithmetic and copies ran while one was open for 9% of the time, Pallas kernels for 41%

profile of v1, /device:TPU:0, one launch (start us, length us, event | category | flops | bytes accessed | tf_op | source)
XLA Modules:
  0.0 382.8 jit_solution(13787728135335139094)
XLA Ops:
  19.7 6.8 %shard_map.466 = (f32[577,1024]{1,0:T(8,128)}, bf16[577,1024]{1,0:T(8,128)(2,1)}, f32[577,1024]{1,0:T(8,128)}, bf16[577,1024]{1,0:T(8,128)(2,1)}, f32[2,1024]{1,...) custom-call(s32[8]{0:T(128)} %broadcast_xor_fusion.order, f32[577,1024]{1,0:T(8,128)} %tok.1, f32[577,1024]{1,0:T(8,128)} %cot.1, ...), custom_call_target="tpu_custom_call" | custom-call | tf_op jit(solution)/shard_map/pallas_call | solution.py:607
  26.5 9.6 %collective-permute-done.1 = bf16[144,1024]{1,0:T(8,128)(2,1)S(1)} collective-permute-done((bf16[144,1024]{1,0:T(8,128)(2,1)S(1)}, bf16[144,1024]{1,0:T(8,128)(2,1)S(1)}, u32[]{:S(2)}, u32[]{:S(2)}) %collective-permute-start.1) | collective-permute-done | bytes 294944 | tf_op jit(solution)/shard_map/ppermute | solution.py:498
  40.2 6.7 %collective-permute-start.5 = (bf16[128,1024]{1,0:T(8,128)(2,1)S(1)}, bf16[128,1024]{1,0:T(8,128)(2,1)S(1)}, u32[]{:S(2)}, u32[]{:S(2)}) collective-permute-start(bf16[128,1024]{1,0:T(8,128)(2,1)S(1)} %convert_element_type.177), channel_id=1, source_target_pairs={{0,1},{1,2},{2,3},{3,0},{4,5},{5,6},{6,7},{7,4},{8,9},{9,10},{10,1... | collective-permute-start | bytes 786440 | tf_op jit(solution)/shard_map/ppermute | solution.py:498
  50.8 4.5 %collective-permute-done.5 = bf16[128,1024]{1,0:T(8,128)(2,1)S(1)} collective-permute-done((bf16[128,1024]{1,0:T(8,128)(2,1)S(1)}, bf16[128,1024]{1,0:T(8,128)(2,1)S(1)}, u32[]{:S(2)}, u32[]{:S(2)}) %collective-permute-start.5) | collective-permute-done | bytes 262176 | tf_op jit(solution)/shard_map/ppermute | solution.py:498
  55.3 8.9 %collective-permute-done.6 = bf16[128,1024]{1,0:T(8,128)(2,1)S(1)} collective-permute-done((bf16[128,1024]{1,0:T(8,128)(2,1)S(1)}, bf16[128,1024]{1,0:T(8,128)(2,1)S(1)}, u32[]{:S(2)}, u32[]{:S(2)}) %collective-permute-start.6) | collective-permute-done | bytes 262176 | tf_op jit(solution)/shard_map/ppermute | solution.py:498
  66.9 12.4 %collective-permute-done.8.refs_5_.refs_7_ = bf16[2,128,1024]{2,1,0:T(8,128)(2,1)S(1)} collective-permute-done((bf16[2,128,1024]{2,1,0:T(8,128)(2,1)S(1)}, bf16[2,128,1024]{2,1,0:T(8,128)(2,1)S(1)}, u32[]{:S(2)}, u32[]{:S(2)}) %collective-permute-start.8) | collective-permute-done | bytes 524320 | tf_op jit(solution)/shard_map/ppermute | solution.py:494
  84.4 6.1 %collective-permute-start.17 = (bf16[128,1024]{1,0:T(8,128)(2,1)S(1)}, bf16[128,1024]{1,0:T(8,128)(2,1)}, u32[]{:S(2)}, u32[]{:S(2)}) collective-permute-start(bf16[128,1024]{1,0:T(8,128)(2,1)S(1)} %bitcast.80), channel_id=1, source_target_pairs={{0,1},{1,2},{2,3},{3,0},{4,5},{5,6},{6,7},{7,4},{8,9},{9,10},{10,1... | collective-permute-start | bytes 786440 | tf_op jit(solution)/shard_map/ppermute | solution.py:498
  93.4 18.9 %shard_map.467 = (bf16[4,577,768]{2,1,0:T(8,128)(2,1)}, bf16[4,577,256]{2,1,0:T(8,128)(2,1)}, f32[4,8,577]{2,1,0:T(8,128)}) custom-call(bf16[577,1024]{1,0:T(8,128)(2,1)} %get-tuple-element.363.refs_0_.refs_3_.x, f32[4,1,768]{2,1,0:T(1,128)} %slice.237.refs_1_, bf16[4,128,1024]{2,1,0:T(8,128)(2,1)} %copy-done, bf16[4,128,1024]{2,1,0:T(8,128)(2,1)} %copy-done.1, ...), custom_call_target="tpu_custom_call" | custom-call | tf_op jit(solution)/shard_map/pallas_call | solution.py:130
  116.7 7.8 %shard_map.468 = (f32[577,1024]{1,0:T(8,128)}, bf16[577,1024]{1,0:T(8,128)(2,1)}) custom-call(bf16[4,577,256]{2,1,0:T(8,128)(2,1)} %get-tuple-element.355.refs_0_.inner, f32[577,1024]{1,0:T(8,128)} %get-tuple-element.284.refs_1_, f32[2,1024]{1,0:T(2,128)} %get-tuple-element.285.refs_2_.refs_5_.refs_3_, f32[4,1024]{1,0:T(4,128)} %get-tuple-element.286.refs_3_.refs_6_, ...), custom_call_target="tpu_custom_call" | custom-call | tf_op jit(solution)/shard_map/pallas_call | solution.py:130
  135.4 14.8 %shard_map.469 = (bf16[4,577,1024]{2,1,0:T(8,128)(2,1)}, bf16[4,577,1024]{2,1,0:T(8,128)(2,1)}, bf16[4,512,1024]{2,1,0:T(8,128)(2,1)}) custom-call(bf16[577,1024]{1,0:T(8,128)(2,1)} %get-tuple-element.289.refs_0_.refs_7_.x, f32[4,1,1024]{2,1,0:T(1,128)} %slice.238.refs_1_, bf16[577,1024]{1,0:T(8,128)(2,1)} %get-tuple-element.310.refs_2_.x.refs_0_, ...), custom_call_target="tpu_custom_call" | custom-call | tf_op jit(solution)/shard_map/pallas_call | solution.py:130
  150.2 3.7 collective-permute-done.25.refs_9_
  158.7 6.8 %collective-permute-done.31.other = bf16[4,512,1024]{2,1,0:T(8,128)(2,1)S(1)} collective-permute-done((bf16[4,512,1024]{2,1,0:T(8,128)(2,1)}, bf16[4,512,1024]{2,1,0:T(8,128)(2,1)S(1)}, u32[]{:S(2)}, u32[]{:S(2)}) %collective-permute-start.31) | collective-permute-done | bytes 4194336 | tf_op jit(solution)/shard_map/ppermute | solution.py:494
  167.5 8.1 %shard_map.470 = (bf16[4,128,1024]{2,1,0:T(8,128)(2,1)}, bf16[4,128,1024]{2,1,0:T(8,128)(2,1)}, bf16[4,128,1024]{2,1,0:T(8,128)(2,1)}, bf16[2,128,1024]{2,1,0:T(8,128)(2,1)}, bf16[2,128,1024]{2,1,0:T(8,128)(2,1)}) custom-call(bf16[577,1024]{1,0:T(8,128)(2,1)} %get-tuple-element.310.refs_2_.x.refs_0_, bf16[4,577,1024]{2,1,0:T(8,128)(2,1)} %get-tuple-element.301.inner.refs_2_, ...), custom_call_target="tpu_custom_call" | custom-call | tf_op jit(solution)/shard_map/pallas_call | solution.py:130
  179.4 31.4 %shard_map.471 = (bf16[4,577,1024]{2,1,0:T(8,128)(2,1)}, f32[4,1,1024]{2,1,0:T(1,128)}, bf16[4,512,1024]{2,1,0:T(8,128)(2,1)}, f32[577,1024]{1,0:T(8,128)}, f32[...) custom-call(s32[8]{0:T(128)} %broadcast_xor_fusion.order, ...), custom_call_target="tpu_custom_call" | custom-call | tf_op jit(solution)/shard_map/pallas_call | solution.py:130
  211.0 4.6 %shard_map.472 = bf16[4,512,256]{2,1,0:T(8,128)(2,1)} custom-call(bf16[577,1024]{1,0:T(8,128)(2,1)} %get-tuple-element.344.x.refs_0_, bf16[4,577,256]{2,1,0:T(8,128)(2,1)} %get-tuple-element.355.refs_0_.inner), custom_call_target="tpu_custom_call" | custom-call | tf_op jit(solution)/shard_map/pallas_call | solution.py:130
  220.4 8.0 %shard_map.473 = (bf16[4,128,1024]{2,1,0:T(8,128)(2,1)}, bf16[4,128,1024]{2,1,0:T(8,128)(2,1)}, bf16[4,128,1024]{2,1,0:T(8,128)(2,1)}, bf16[2,128,1024]{2,1,0:T(8,128)(2,1)}, bf16[2,128,1024]{2,1,0:T(8,128)(2,1)}) custom-call(bf16[577,1024]{1,0:T(8,128)(2,1)} %get-tuple-element.289.refs_0_.refs_7_.x, bf16[4,577,1024]{2,1,0:T(8,128)(2,1)} %get-tuple-element.329.inner, ...), custom_call_target="tpu_custom_call" | custom-call | tf_op jit(solution)/shard_map/pallas_call | solution.py:130
  230.8 29.5 %shard_map.474 = (bf16[4,577,768]{2,1,0:T(8,128)(2,1)}, f32[4,2,256]{2,1,0:T(2,128)}, bf16[4,512,768]{2,1,0:T(8,128)(2,1)}) custom-call(bf16[577,1024]{1,0:T(8,128)(2,1)} %get-tuple-element.344.x.refs_0_, bf16[4,577,768]{2,1,0:T(8,128)(2,1)} %get-tuple-element.345.refs_1_, f32[4,8,577]{2,1,0:T(8,128)} %get-tuple-element.346.refs_2_, ...), custom_call_target="tpu_custom_call" | custom-call | tf_op jit(solution)/shard_map/pallas_call | solution.py:130
  271.9 4.9 %shard_map.475 = (bf16[4,128,256]{2,1,0:T(8,128)(2,1)}, bf16[4,128,256]{2,1,0:T(8,128)(2,1)}, bf16[4,128,256]{2,1,0:T(8,128)(2,1)}, bf16[2,128,256]{2,1,0:T(8,128)(2,1)}, bf16[2,128,256]{2,1,0:T(8,128)(2,1)}) custom-call(bf16[577,1024]{1,0:T(8,128)(2,1)} %get-tuple-element.344.x.refs_0_, bf16[4,577,256]{2,1,0:T(8,128)(2,1)} %get-tuple-element.355.refs_0_.inner, ...), custom_call_target="tpu_custom_call" | custom-call | tf_op jit(solution)/shard_map/pallas_call | solution.py:130
  278.5 6.9 %shard_map.476 = (bf16[4,128,768]{2,1,0:T(8,128)(2,1)}, bf16[4,128,768]{2,1,0:T(8,128)(2,1)}, bf16[4,128,768]{2,1,0:T(8,128)(2,1)}, bf16[2,128,768]{2,1,0:T(8,128)(2,1)}, bf16[2,128,768]{2,1,0:T(8,128)(2,1)}) custom-call(bf16[577,1024]{1,0:T(8,128)(2,1)} %get-tuple-element.363.refs_0_.refs_3_.x, bf16[4,577,768]{2,1,0:T(8,128)(2,1)} %get-tuple-element.371.inner.refs_0_, ...), custom_call_target="tpu_custom_call" | custom-call | tf_op jit(solution)/shard_map/pallas_call | solution.py:130
  287.9 13.2 %shard_map.477 = (f32[577,1024]{1,0:T(8,128)}, f32[2,1024]{1,0:T(2,128)}) custom-call(s32[8]{0:T(128)} %broadcast_xor_fusion.order, bf16[4,577,768]{2,1,0:T(8,128)(2,1)} %get-tuple-element.371.inner.refs_0_, f32[577,1024]{1,0:T(8,128)} %get-tuple-element.284.refs_1_, f32[577,1024]{1,0:T(8,128)} %get-tuple-element.372.refs_2_, ...), custom_call_target="tpu_custom_call" | custom-call | tf_op jit(solution)/shard_map/pallas_call | solution.py:130
  311.3 3.6 collective-permute-start.57
  322.4 12.3 %reduce-scatter.4.cloned.1.call-done = bf16[1,128,1024]{2,1,0:T(8,128)(2,1)} async-done(((bf16[4,128,1024]{2,1,0:T(8,128)(2,1)}), bf16[1,128,1024]{2,1,0:T(8,128)(2,1)}) %reduce-scatter.4.cloned.1.call-update) | async-done | bytes 262160 | tf_op jit(solution)/shard_map/reduce_scatter | solution.py:546
  345.7 4.4 %collective-permute-start.58 = (bf16[128,768]{1,0:T(8,128)(2,1)S(1)}, bf16[128,768]{1,0:T(8,128)(2,1)S(1)}, u32[]{:S(2)}, u32[]{:S(2)}) collective-permute-start(bf16[128,768]{1,0:T(8,128)(2,1)S(1)} %get-tuple-element.429), channel_id=1, source_target_pairs={{0,3},{1,0},{2,1},{3,2},{4,7},{5,4},{6,5},{7,6},{8,11},{9,8},{10,9... | collective-permute-start | bytes 589832 | tf_op jit(solution)/shard_map/ppermute | solution.py:498
  358.9 12.3 %collective-permute-done.59 = bf16[128,768]{1,0:T(8,128)(2,1)S(1)} collective-permute-done((bf16[128,768]{1,0:T(8,128)(2,1)S(1)}, bf16[128,768]{1,0:T(8,128)(2,1)S(1)}, u32[]{:S(2)}, u32[]{:S(2)}) %collective-permute-start.59) | collective-permute-done | bytes 196640 | tf_op jit(solution)/shard_map/ppermute | solution.py:498
  (383 shorter events, 121.3 us)
Async XLA Ops:
  7.2 310.3 %reduce-scatter.6.cloned.1.call-start = ((), (), s32[]{:S(2)}) async-start(), calls=%async_computation.4 | async-start | bytes 1310720 | tf_op jit(solution)/shard_map/reduce_scatter | solution.py:546
  14.3 21.8 %collective-permute-start.1 = (bf16[144,1024]{1,0:T(8,128)(2,1)S(1)}, bf16[144,1024]{1,0:T(8,128)(2,1)S(1)}, u32[]{:S(2)}, u32[]{:S(2)}) collective-permute-start(bf16[144,1024]{1,0:T(8,128)(2,1)S(1)} %concatenate.41), channel_id=1, source_target_pairs={{0,2},{1,3},{2,0},{3,1},{4,6},{5,7},{6,4},{7,5},{8,10},{9,11},{10,... | collective-permute-start | bytes 884744 | tf_op jit(solution)/shard_map/ppermute | solution.py:498
  37.1 27.1 %collective-permute-start.3 = (bf16[4,128,1024]{2,1,0:T(8,128)(2,1)S(1)}, bf16[4,128,1024]{2,1,0:T(8,128)(2,1)S(1)}, u32[]{:S(2)}, u32[]{:S(2)}) collective-permute-start(bf16[4,128,1024]{2,1,0:T(8,128)(2,1)S(1)} %pad_maximum_fusion.refs_2_.refs_4_), channel_id=1, source_target_pairs={{0,8},{4,12},{8,0},{12,4},{16,24},{20,28},{24,16},{28,20},{1,9},{5... | collective-permute-start | bytes 3145736 | tf_op jit(solution)/shard_map/ppermute | solution.py:494
  38.6 25.6 %collective-permute-start.4 = (bf16[4,128,1024]{2,1,0:T(8,128)(2,1)S(1)}, bf16[4,128,1024]{2,1,0:T(8,128)(2,1)S(1)}, u32[]{:S(2)}, u32[]{:S(2)}) collective-permute-start(bf16[4,128,1024]{2,1,0:T(8,128)(2,1)S(1)} %pad_maximum_fusion.refs_2_.refs_4_), channel_id=1, source_target_pairs={{0,16},{4,20},{8,24},{12,28},{16,0},{20,4},{24,8},{28,12},{1,17},{... | collective-permute-start | bytes 3145736 | tf_op jit(solution)/shard_map/ppermute | solution.py:494
  79.6 32.7 %collective-permute-start.13 = (bf16[4,128,1024]{2,1,0:T(8,128)(2,1)S(1)}, bf16[4,128,1024]{2,1,0:T(8,128)(2,1)S(1)}, u32[]{:S(2)}, u32[]{:S(2)}) collective-permute-start(bf16[4,128,1024]{2,1,0:T(8,128)(2,1)S(1)} %pad_maximum_fusion.1.refs_3_.refs_18_), channel_id=1, source_target_pairs={{0,8},{4,12},{8,0},{12,4},{16,24},{20,28},{24,16},{28,20},{1,9},{5... | collective-permute-start | bytes 3145736 | tf_op jit(solution)/shard_map/ppermute | solution.py:494
  80.2 32.1 %collective-permute-start.14 = (bf16[4,128,1024]{2,1,0:T(8,128)(2,1)S(1)}, bf16[4,128,1024]{2,1,0:T(8,128)(2,1)S(1)}, u32[]{:S(2)}, u32[]{:S(2)}) collective-permute-start(bf16[4,128,1024]{2,1,0:T(8,128)(2,1)S(1)} %pad_maximum_fusion.1.refs_3_.refs_18_), channel_id=1, source_target_pairs={{0,16},{4,20},{8,24},{12,28},{16,0},{20,4},{24,8},{28,12},{1,17},{... | collective-permute-start | bytes 3145736 | tf_op jit(solution)/shard_map/ppermute | solution.py:494
  84.4 28.0 %collective-permute-start.17 = (bf16[128,1024]{1,0:T(8,128)(2,1)S(1)}, bf16[128,1024]{1,0:T(8,128)(2,1)}, u32[]{:S(2)}, u32[]{:S(2)}) collective-permute-start(bf16[128,1024]{1,0:T(8,128)(2,1)S(1)} %bitcast.80), channel_id=1, source_target_pairs={{0,1},{1,2},{2,3},{3,0},{4,5},{5,6},{6,7},{7,4},{8,9},{9,10},{10,1... | collective-permute-start | bytes 786440 | tf_op jit(solution)/shard_map/ppermute | solution.py:498
  90.4 21.9 %collective-permute-start.18 = (bf16[128,1024]{1,0:T(8,128)(2,1)S(1)}, bf16[128,1024]{1,0:T(8,128)(2,1)}, u32[]{:S(2)}, u32[]{:S(2)}) collective-permute-start(bf16[128,1024]{1,0:T(8,128)(2,1)S(1)} %bitcast.81), channel_id=1, source_target_pairs={{0,2},{1,3},{2,0},{3,1},{4,6},{5,7},{6,4},{7,5},{8,10},{9,11},{10,... | collective-permute-start | bytes 786440 | tf_op jit(solution)/shard_map/ppermute | solution.py:498
  129.4 24.5 %collective-permute-start.25 = (bf16[4,128,1024]{2,1,0:T(8,128)(2,1)S(1)}, bf16[4,128,1024]{2,1,0:T(8,128)(2,1)S(1)}, u32[]{:S(2)}, u32[]{:S(2)}) collective-permute-start(bf16[4,128,1024]{2,1,0:T(8,128)(2,1)S(1)} %pad_maximum_fusion.2.refs_8_), channel_id=1, source_target_pairs={{0,8},{4,12},{8,0},{12,4},{16,24},{20,28},{24,16},{28,20},{1,9},{5... | collective-permute-start | bytes 3145736 | tf_op jit(solution)/shard_map/ppermute | solution.py:494
  130.9 24.1 %collective-permute-start.26 = (bf16[4,128,1024]{2,1,0:T(8,128)(2,1)S(1)}, bf16[4,128,1024]{2,1,0:T(8,128)(2,1)S(1)}, u32[]{:S(2)}, u32[]{:S(2)}) collective-permute-start(bf16[4,128,1024]{2,1,0:T(8,128)(2,1)S(1)} %pad_maximum_fusion.2.refs_8_), channel_id=1, source_target_pairs={{0,16},{4,20},{8,24},{12,28},{16,0},{20,4},{24,8},{28,12},{1,17},{... | collective-permute-start | bytes 3145736 | tf_op jit(solution)/shard_map/ppermute | solution.py:494
  176.2 34.6 %collective-permute-start.37 = (bf16[2,128,1024]{2,1,0:T(8,128)(2,1)}, bf16[2,128,1024]{2,1,0:T(8,128)(2,1)S(1)}, u32[]{:S(2)}, u32[]{:S(2)}) collective-permute-start(bf16[2,128,1024]{2,1,0:T(8,128)(2,1)} %get-tuple-element.319), channel_id=1, source_target_pairs={{0,16},{4,20},{8,24},{12,28},{16,0},{20,4},{24,8},{28,12},{1,17},{... | collective-permute-start | bytes 1572872 | tf_op jit(solution)/shard_map/ppermute | solution.py:494
  177.0 33.8 %collective-permute-start.38 = (bf16[2,128,1024]{2,1,0:T(8,128)(2,1)}, bf16[2,128,1024]{2,1,0:T(8,128)(2,1)S(1)}, u32[]{:S(2)}, u32[]{:S(2)}) collective-permute-start(bf16[2,128,1024]{2,1,0:T(8,128)(2,1)} %get-tuple-element.320), channel_id=1, source_target_pairs={{0,8},{4,12},{8,0},{12,4},{16,24},{20,28},{24,16},{28,20},{1,9},{5... | collective-permute-start | bytes 1572872 | tf_op jit(solution)/shard_map/ppermute | solution.py:494
  216.0 44.3 %collective-permute-start.43 = (bf16[4,128,1024]{2,1,0:T(8,128)(2,1)S(1)}, bf16[4,128,1024]{2,1,0:T(8,128)(2,1)}, u32[]{:S(2)}, u32[]{:S(2)}) collective-permute-start(bf16[4,128,1024]{2,1,0:T(8,128)(2,1)S(1)} %pad_maximum_fusion.4), channel_id=1, source_target_pairs={{0,16},{4,20},{8,24},{12,28},{16,0},{20,4},{24,8},{28,12},{1,17},{... | collective-permute-start | bytes 3145736 | tf_op jit(solution)/shard_map/ppermute | solution.py:494
  217.4 42.9 %collective-permute-start.42 = (bf16[4,128,1024]{2,1,0:T(8,128)(2,1)S(1)}, bf16[4,128,1024]{2,1,0:T(8,128)(2,1)}, u32[]{:S(2)}, u32[]{:S(2)}) collective-permute-start(bf16[4,128,1024]{2,1,0:T(8,128)(2,1)S(1)} %pad_maximum_fusion.3), channel_id=1, source_target_pairs={{0,8},{4,12},{8,0},{12,4},{16,24},{20,28},{24,16},{28,20},{1,9},{5... | collective-permute-start | bytes 3145736 | tf_op jit(solution)/shard_map/ppermute | solution.py:494
  228.4 32.0 %collective-permute-start.44 = (bf16[4,512,256]{2,1,0:T(8,128)(2,1)S(1)}, bf16[4,512,256]{2,1,0:T(8,128)(2,1)S(1)}, u32[]{:S(2)}, u32[]{:S(2)}) collective-permute-start(bf16[4,512,256]{2,1,0:T(8,128)(2,1)S(1)} %copy-done.33), channel_id=1, source_target_pairs={{0,4},{4,0},{8,12},{12,8},{16,20},{20,16},{24,28},{28,24},{1,5},{5... | collective-permute-start | bytes 3145736 | tf_op jit(solution)/shard_map/ppermute | solution.py:494
  228.5 31.8 %collective-permute-start.40 = (bf16[2,128,1024]{2,1,0:T(8,128)(2,1)}, bf16[2,128,1024]{2,1,0:T(8,128)(2,1)S(1)}, u32[]{:S(2)}, u32[]{:S(2)}) collective-permute-start(bf16[2,128,1024]{2,1,0:T(8,128)(2,1)} %get-tuple-element.338), channel_id=1, source_target_pairs={{0,16},{4,20},{8,24},{12,28},{16,0},{20,4},{24,8},{28,12},{1,17},{... | collective-permute-start | bytes 1572872 | tf_op jit(solution)/shard_map/ppermute | solution.py:494
  229.5 30.9 %collective-permute-start.41 = (bf16[2,128,1024]{2,1,0:T(8,128)(2,1)}, bf16[2,128,1024]{2,1,0:T(8,128)(2,1)}, u32[]{:S(2)}, u32[]{:S(2)}) collective-permute-start(bf16[2,128,1024]{2,1,0:T(8,128)(2,1)} %get-tuple-element.339), channel_id=1, source_target_pairs={{0,8},{4,12},{8,0},{12,4},{16,24},{20,28},{24,16},{28,20},{1,9},{5... | collective-permute-start | bytes 1572872 | tf_op jit(solution)/shard_map/ppermute | solution.py:494
  265.2 36.9 %collective-permute-start.49 = (bf16[4,128,1024]{2,1,0:T(8,128)(2,1)}, bf16[4,128,1024]{2,1,0:T(8,128)(2,1)}, u32[]{:S(2)}, u32[]{:S(2)}) collective-permute-start(bf16[4,128,1024]{2,1,0:T(8,128)(2,1)} %pad_maximum_fusion.6), channel_id=1, source_target_pairs={{0,16},{4,20},{8,24},{12,28},{16,0},{20,4},{24,8},{28,12},{1,17},{... | collective-permute-start | bytes 3145736 | tf_op jit(solution)/shard_map/ppermute | solution.py:494
  267.5 34.6 %collective-permute-start.48 = (bf16[4,128,1024]{2,1,0:T(8,128)(2,1)}, bf16[4,128,1024]{2,1,0:T(8,128)(2,1)}, u32[]{:S(2)}, u32[]{:S(2)}) collective-permute-start(bf16[4,128,1024]{2,1,0:T(8,128)(2,1)} %pad_maximum_fusion.5), channel_id=1, source_target_pairs={{0,8},{4,12},{8,0},{12,4},{16,24},{20,28},{24,16},{28,20},{1,9},{5... | collective-permute-start | bytes 3145736 | tf_op jit(solution)/shard_map/ppermute | solution.py:494
  271.8 63.0 %reduce-scatter.4.cloned.1.call-start = ((), (), s32[]{:S(2)}) async-start(), calls=%async_computation.3 | async-start | bytes 1310720 | tf_op jit(solution)/shard_map/reduce_scatter | solution.py:546
  306.9 65.6 %reduce-scatter.8.cloned.1.call-start = ((), (), s32[]{:S(2)}) async-start(), calls=%async_computation.5 | async-start | bytes 327680 | tf_op jit(solution)/shard_map/reduce_scatter | solution.py:546
  308.8 27.5 %collective-permute-start.50 = (bf16[4,128,768]{2,1,0:T(8,128)(2,1)S(1)}, bf16[4,128,768]{2,1,0:T(8,128)(2,1)}, u32[]{:S(2)}, u32[]{:S(2)}) collective-permute-start(bf16[4,128,768]{2,1,0:T(8,128)(2,1)S(1)} %pad_maximum_fusion.9), channel_id=1, source_target_pairs={{0,8},{4,12},{8,0},{12,4},{16,24},{20,28},{24,16},{28,20},{1,9},{5... | collective-permute-start | bytes 2359304 | tf_op jit(solution)/shard_map/ppermute | solution.py:494
  310.2 26.1 %collective-permute-start.51 = (bf16[4,128,768]{2,1,0:T(8,128)(2,1)S(1)}, bf16[4,128,768]{2,1,0:T(8,128)(2,1)}, u32[]{:S(2)}, u32[]{:S(2)}) collective-permute-start(bf16[4,128,768]{2,1,0:T(8,128)(2,1)S(1)} %pad_maximum_fusion.10), channel_id=1, source_target_pairs={{0,16},{4,20},{8,24},{12,28},{16,0},{20,4},{24,8},{28,12},{1,17},{... | collective-permute-start | bytes 2359304 | tf_op jit(solution)/shard_map/ppermute | solution.py:494
  350.0 21.2 %collective-permute-start.59 = (bf16[128,768]{1,0:T(8,128)(2,1)S(1)}, bf16[128,768]{1,0:T(8,128)(2,1)S(1)}, u32[]{:S(2)}, u32[]{:S(2)}) collective-permute-start(bf16[128,768]{1,0:T(8,128)(2,1)S(1)} %get-tuple-element.430), channel_id=1, source_target_pairs={{0,2},{1,3},{2,0},{3,1},{4,6},{5,7},{6,4},{7,5},{8,10},{9,11},{10,... | collective-permute-start | bytes 589832 | tf_op jit(solution)/shard_map/ppermute | solution.py:498
  (122 other events, 1351.7 us)
Sparse Core Ops, SparseCore 0:
  271.9 28.0 reduce-scatter.5
  307.1 27.6 reduce-scatter.3
  345.8 26.6 reduce-scatter.7

commit v2 on v1

--- a/solution.py
+++ b/solution.py
@@ -116,6 +116,18 @@
 
 def once_spec(*shape):
     return pl.BlockSpec(shape, lambda n, *s: (0,) * len(shape), pipeline_mode=pl.Buffered(1))
+
+
+def late_spec():
+    return pl.BlockSpec(memory_space=pl.ANY)
+
+
+def late_scratch(rows):
+    return [pltpu.VMEM((rows, D), full), pltpu.VMEM((rows, D), full), pltpu.SemaphoreType.DMA((2,))]
+
+
+def late_copies(sources, targets, sems):
+    return [pltpu.make_async_copy(sources[at], targets[at], sems.at[at]) for at in range(2)]
 
 
 def twin_half(rows):
@@ -314,13 +326,16 @@
     grad, slope, active, middle, cot, gains, shifts, normed = refs[:8]
     shrink_own, shrink_twin = refs[8:13], refs[13:18]
     expand_own, expand_twin = refs[18:23], refs[23:28]
-    inner, sums, outer, layer, out, out_low, two_sums, total, result = refs[28:]
+    inner, sums, outer, layer, out, out_low, two_sums, total, result, middle_late, cot_late, sems = refs[28:]
     n = pl.program_id(0)
+    copies = late_copies((middle, cot), (middle_late, cot_late), sems)
 
     @pl.when(n == 0)
     def _():
+        for copy in copies:
+            copy.start()
         total[...] = jnp.zeros_like(total)
-        result[...] = middle[...] + shifts[3:4]
+        result[...] = jnp.zeros_like(result)
 
     own, twin = assemble(shrink_own, groups), assemble(shrink_twin, groups)
     value = (dot_nn(grad[:, :HALF], own) + dot_nn(grad[:, HALF:], twin)) * slope[0].astype(full)
@@ -334,15 +349,17 @@
 
     @pl.when(n == groups - 1)
     def _():
-        part, gain_sum, shift_sum = norm_back(middle[...], total[...], gains[1:2])
-        grad_out = cot[...] + part
+        for copy in copies:
+            copy.wait()
+        part, gain_sum, shift_sum = norm_back(middle_late[...], total[...], gains[1:2])
+        grad_out = cot_late[...] + part
         out[...] = grad_out
         out_low[...] = grad_out.astype(low)
         grad_sum = jnp.sum(grad_out, axis=0, keepdims=True)
         for at in range(BLOCKS):
             place = lane_block(order, at)
             cols = slice(at * LANES, (at + 1) * LANES)
-            layer[:, place] = result[:, cols]
+            layer[:, place] = result[:, cols] + middle_late[:, cols] + shifts[3:4, cols]
             two_sums[0:1, place] = gain_sum[:, cols]
             two_sums[1:2, place] = shift_sum[:, cols]
             two_sums[2:3, place] = grad_sum[:, cols]
@@ -356,7 +373,8 @@
     return grouped(
         functools.partial(hidden_back_kernel, groups),
         groups,
-        [once, group, group, once, once, whole_spec(2, D), whole_spec(4, D), twin_half(rows)] + pieces * 4,
+        [once, group, group, late_spec(), late_spec(), whole_spec(2, D), whole_spec(4, D), twin_half(rows)]
+        + pieces * 4,
         [group, group_spec(1, width), group_spec(HALF, width), once, once, once, whole_spec(3, D)],
         [
             struct((groups, rows, width), low),
@@ -382,7 +400,7 @@
             *own,
             *twin,
         ),
-        scratch=[pltpu.VMEM((rows, D), full), pltpu.VMEM((rows, D), full)],
+        scratch=[pltpu.VMEM((rows, D), full), pltpu.VMEM((rows, D), full)] + late_scratch(rows),
         prefetch=1,
     )
 
@@ -438,19 +456,24 @@
 def norm_one_kernel(groups, order, *refs):
     inner, tok, grad, gains = refs[:4]
     own, twin = refs[4:9], refs[9:14]
-    out, sums, total = refs[14:]
+    out, sums, total, tok_late, grad_late, sems = refs[14:]
     n = pl.program_id(0)
+    copies = late_copies((tok, grad), (tok_late, grad_late), sems)
 
     @pl.when(n == 0)
     def _():
+        for copy in copies:
+            copy.start()
         total[...] = jnp.zeros_like(total)
 
     add_parts(groups, inner, own, twin, total)
 
     @pl.when(n == groups - 1)
     def _():
-        part, gain_sum, shift_sum = norm_back(tok[...], total[...], gains[0:1])
-        result = grad[...] + part
+        for copy in copies:
+            copy.wait()
+        part, gain_sum, shift_sum = norm_back(tok_late[...], total[...], gains[0:1])
+        result = grad_late[...] + part
         for at in range(BLOCKS):
             place = lane_block(order, at)
             cols = slice(at * LANES, (at + 1) * LANES)
@@ -465,11 +488,13 @@
     return grouped(
         functools.partial(norm_one_kernel, groups),
         groups,
-        [group_spec(rows, width), whole, whole, whole_spec(2, D)] + piece_specs(own, width) + piece_specs(twin, width),
+        [group_spec(rows, width), late_spec(), late_spec(), whole_spec(2, D)]
+        + piece_specs(own, width)
+        + piece_specs(twin, width),
         [whole, whole_spec(2, D)],
         [struct((rows, D), full), struct((2, D), full)],
         (order, inner, values, grad, gains, *own, *twin),
-        scratch=[pltpu.VMEM((rows, D), full)],
+        scratch=[pltpu.VMEM((rows, D), full)] + late_scratch(rows),
         prefetch=1,
     )
 
@@ -786,6 +811,8 @@
         small = small + swap(small, 4)
         t_back = [turn(t_last[step], -step) for step in range(1, 4)]
         output_grad = narrow_scatter(o_pieces[0], o_over_x, o_over_y, steps)
+        output_done = turned_adam(1.0, output_grad, output_weight, output_first, output_second)
+        t_back, output_done = fence(t_back, output_done)
         triple_grad = last_sum(t_last[0], t_back)
     else:
         small = lax.psum(small, ("wide", "narrow"))
@@ -796,7 +823,7 @@
     triple_gradient = jnp.stack([triple_grad[:, at * local : (at + 1) * local] for at in range(3)], axis=1)
     if not tuned:
         shrink_done = turned_adam(0.05, shrink_grad, shrink_weight, shrink_first, shrink_second)
-    output_done = turned_adam(1.0, output_grad, output_weight, output_first, output_second)
+        output_done = turned_adam(1.0, output_grad, output_weight, output_first, output_second)
     gains_gradient = small[0:2]
     shifts_gradient = small[2:6]
     heads_gradient = lax.dynamic_slice_in_dim(small[6:8], at_narrow * local, local, 1)

time: 388 us -> 389 us (level)
    reduce_scatter x3, waiting for transfers between devices: 12.3 us -> 25.7 us  [narrow_scatter(): lax.psum_scatter(jnp.stack(parts), 'narrow', scatter_dimension=0, tiled=F...]
    ppermute x12, waiting for transfers between devices: 35.3 us -> 23 us  [turn(): lax.ppermute(values, 'narrow', [(at, (at + step) % 4) for at in range(4)])]
  transfers between devices with their start and end apart: 67 -> 67, of which waited for: 20 -> 21; matrix products, arithmetic and copies ran while one was open for 9% -> 9% of each run, Pallas kernels for 41% -> 41%
where the time goes in v2:
time: 389 us; the launch traced here: 384 us
  Pallas kernels  158 us (41%)
  waiting for transfers between devices  86.3 us (22%)
  starting transfers between devices  71.5 us (18%)
  other arithmetic  30.1 us (8%)
  local copies, waits for them, and re-layouts  22.6 us (6%)
  between operations  15.4 us (4%)
    pallas_call x11, Pallas kernels, grouped(): pl.pallas_call(kernel, grid_spec=pltpu.PrefetchScalarGridSpec(num_scalar_...  146 us
    ppermute x50, waiting for transfers between devices, swap(): return lax.ppermute(values, 'wide', [(at, at ^ bit) for at in range(8)])  36.2 us
    ppermute x50, starting transfers between devices, swap(): return lax.ppermute(values, 'wide', [(at, at ^ bit) for at in range(8)])  34.6 us
    ppermute x12, starting transfers between devices, turn(): lax.ppermute(values, 'narrow', [(at, (at + step) % 4) for at in range(4)])  30.3 us
    reduce_scatter x3, waiting for transfers between devices, narrow_scatter(): lax.psum_scatter(jnp.stack(parts), 'narrow', scatter_dimension=0, tiled=F...  25.7 us
    ppermute x12, waiting for transfers between devices, turn(): lax.ppermute(values, 'narrow', [(at, (at + step) % 4) for at in range(4)])  23 us
    unnamed x162, local copies, waits for them, and re-layouts  12.4 us
  transfers between devices with their start and end apart: 67, of which 21 were waited for; matrix products, arithmetic and copies ran while one was open for 9% of the time, Pallas kernels for 41%

profile of v2, /device:TPU:0, one launch (start us, length us, event | category | flops | bytes accessed | tf_op | source)
XLA Modules:
  0.0 383.6 jit_solution(17291829776903938099)
XLA Ops:
  19.7 6.8 %shard_map.466 = (f32[577,1024]{1,0:T(8,128)}, bf16[577,1024]{1,0:T(8,128)(2,1)}, f32[577,1024]{1,0:T(8,128)}, bf16[577,1024]{1,0:T(8,128)(2,1)}, f32[2,1024]{1,...) custom-call(s32[8]{0:T(128)} %broadcast_xor_fusion.order, f32[577,1024]{1,0:T(8,128)} %tok.1, f32[577,1024]{1,0:T(8,128)} %cot.1, ...), custom_call_target="tpu_custom_call" | custom-call | tf_op jit(solution)/shard_map/pallas_call | solution.py:632
  26.5 9.6 %collective-permute-done.1 = bf16[144,1024]{1,0:T(8,128)(2,1)S(1)} collective-permute-done((bf16[144,1024]{1,0:T(8,128)(2,1)S(1)}, bf16[144,1024]{1,0:T(8,128)(2,1)S(1)}, u32[]{:S(2)}, u32[]{:S(2)}) %collective-permute-start.1) | collective-permute-done | bytes 294944 | tf_op jit(solution)/shard_map/ppermute | solution.py:523
  40.2 6.7 %collective-permute-start.5 = (bf16[128,1024]{1,0:T(8,128)(2,1)S(1)}, bf16[128,1024]{1,0:T(8,128)(2,1)S(1)}, u32[]{:S(2)}, u32[]{:S(2)}) collective-permute-start(bf16[128,1024]{1,0:T(8,128)(2,1)S(1)} %convert_element_type.177), channel_id=1, source_target_pairs={{0,1},{1,2},{2,3},{3,0},{4,5},{5,6},{6,7},{7,4},{8,9},{9,10},{10,1... | collective-permute-start | bytes 786440 | tf_op jit(solution)/shard_map/ppermute | solution.py:523
  50.8 4.5 %collective-permute-done.5 = bf16[128,1024]{1,0:T(8,128)(2,1)S(1)} collective-permute-done((bf16[128,1024]{1,0:T(8,128)(2,1)S(1)}, bf16[128,1024]{1,0:T(8,128)(2,1)S(1)}, u32[]{:S(2)}, u32[]{:S(2)}) %collective-permute-start.5) | collective-permute-done | bytes 262176 | tf_op jit(solution)/shard_map/ppermute | solution.py:523
  55.3 8.9 %collective-permute-done.6 = bf16[128,1024]{1,0:T(8,128)(2,1)S(1)} collective-permute-done((bf16[128,1024]{1,0:T(8,128)(2,1)S(1)}, bf16[128,1024]{1,0:T(8,128)(2,1)S(1)}, u32[]{:S(2)}, u32[]{:S(2)}) %collective-permute-start.6) | collective-permute-done | bytes 262176 | tf_op jit(solution)/shard_map/ppermute | solution.py:523
  66.9 12.4 %collective-permute-done.8.refs_5_.refs_7_ = bf16[2,128,1024]{2,1,0:T(8,128)(2,1)S(1)} collective-permute-done((bf16[2,128,1024]{2,1,0:T(8,128)(2,1)S(1)}, bf16[2,128,1024]{2,1,0:T(8,128)(2,1)S(1)}, u32[]{:S(2)}, u32[]{:S(2)}) %collective-permute-start.8) | collective-permute-done | bytes 524320 | tf_op jit(solution)/shard_map/ppermute | solution.py:519
  84.4 6.1 %collective-permute-start.17 = (bf16[128,1024]{1,0:T(8,128)(2,1)S(1)}, bf16[128,1024]{1,0:T(8,128)(2,1)}, u32[]{:S(2)}, u32[]{:S(2)}) collective-permute-start(bf16[128,1024]{1,0:T(8,128)(2,1)S(1)} %bitcast.80), channel_id=1, source_target_pairs={{0,1},{1,2},{2,3},{3,0},{4,5},{5,6},{6,7},{7,4},{8,9},{9,10},{10,1... | collective-permute-start | bytes 786440 | tf_op jit(solution)/shard_map/ppermute | solution.py:523
  93.4 18.9 %shard_map.467 = (bf16[4,577,768]{2,1,0:T(8,128)(2,1)}, bf16[4,577,256]{2,1,0:T(8,128)(2,1)}, f32[4,8,577]{2,1,0:T(8,128)}) custom-call(bf16[577,1024]{1,0:T(8,128)(2,1)} %get-tuple-element.369.refs_0_.refs_3_.x, f32[4,1,768]{2,1,0:T(1,128)} %slice.237.refs_1_, bf16[4,128,1024]{2,1,0:T(8,128)(2,1)} %copy-done, bf16[4,128,1024]{2,1,0:T(8,128)(2,1)} %copy-done.1, ...), custom_call_target="tpu_custom_call" | custom-call | tf_op jit(solution)/shard_map/pallas_call | solution.py:142
  116.7 7.8 %shard_map.468 = (f32[577,1024]{1,0:T(8,128)}, bf16[577,1024]{1,0:T(8,128)(2,1)}) custom-call(bf16[4,577,256]{2,1,0:T(8,128)(2,1)} %get-tuple-element.361.refs_0_.inner, f32[577,1024]{1,0:T(8,128)} %get-tuple-element.290.refs_1_, f32[2,1024]{1,0:T(2,128)} %get-tuple-element.291.refs_2_.refs_5_.refs_3_, f32[4,1024]{1,0:T(4,128)} %get-tuple-element.292.refs_3_.refs_6_, ...), custom_call_target="tpu_custom_call" | custom-call | tf_op jit(solution)/shard_map/pallas_call | solution.py:142
  135.4 14.8 %shard_map.469 = (bf16[4,577,1024]{2,1,0:T(8,128)(2,1)}, bf16[4,577,1024]{2,1,0:T(8,128)(2,1)}, bf16[4,512,1024]{2,1,0:T(8,128)(2,1)}) custom-call(bf16[577,1024]{1,0:T(8,128)(2,1)} %get-tuple-element.295.refs_0_.refs_7_.x, f32[4,1,1024]{2,1,0:T(1,128)} %slice.238.refs_1_, bf16[577,1024]{1,0:T(8,128)(2,1)} %get-tuple-element.316.refs_2_.x.refs_0_, ...), custom_call_target="tpu_custom_call" | custom-call | tf_op jit(solution)/shard_map/pallas_call | solution.py:142
  150.2 3.7 collective-permute-done.25.refs_9_
  158.7 6.8 %collective-permute-done.31.other = bf16[4,512,1024]{2,1,0:T(8,128)(2,1)S(1)} collective-permute-done((bf16[4,512,1024]{2,1,0:T(8,128)(2,1)}, bf16[4,512,1024]{2,1,0:T(8,128)(2,1)S(1)}, u32[]{:S(2)}, u32[]{:S(2)}) %collective-permute-start.31) | collective-permute-done | bytes 4194336 | tf_op jit(solution)/shard_map/ppermute | solution.py:519
  167.5 8.1 %shard_map.470 = (bf16[4,128,1024]{2,1,0:T(8,128)(2,1)}, bf16[4,128,1024]{2,1,0:T(8,128)(2,1)}, bf16[4,128,1024]{2,1,0:T(8,128)(2,1)}, bf16[2,128,1024]{2,1,0:T(8,128)(2,1)}, bf16[2,128,1024]{2,1,0:T(8,128)(2,1)}) custom-call(bf16[577,1024]{1,0:T(8,128)(2,1)} %get-tuple-element.316.refs_2_.x.refs_0_, bf16[4,577,1024]{2,1,0:T(8,128)(2,1)} %get-tuple-element.307.inner.refs_2_, ...), custom_call_target="tpu_custom_call" | custom-call | tf_op jit(solution)/shard_map/pallas_call | solution.py:142
  179.4 30.6 %shard_map.471 = (bf16[4,577,1024]{2,1,0:T(8,128)(2,1)}, f32[4,1,1024]{2,1,0:T(1,128)}, bf16[4,512,1024]{2,1,0:T(8,128)(2,1)}, f32[577,1024]{1,0:T(8,128)}, f32[...) custom-call(s32[8]{0:T(128)} %broadcast_xor_fusion.order, ...), custom_call_target="tpu_custom_call" | custom-call | tf_op jit(solution)/shard_map/pallas_call | solution.py:142
  210.2 4.6 %shard_map.472 = bf16[4,512,256]{2,1,0:T(8,128)(2,1)} custom-call(bf16[577,1024]{1,0:T(8,128)(2,1)} %get-tuple-element.350.x.refs_0_, bf16[4,577,256]{2,1,0:T(8,128)(2,1)} %get-tuple-element.361.refs_0_.inner), custom_call_target="tpu_custom_call" | custom-call | tf_op jit(solution)/shard_map/pallas_call | solution.py:142
  219.6 8.0 %shard_map.473 = (bf16[4,128,1024]{2,1,0:T(8,128)(2,1)}, bf16[4,128,1024]{2,1,0:T(8,128)(2,1)}, bf16[4,128,1024]{2,1,0:T(8,128)(2,1)}, bf16[2,128,1024]{2,1,0:T(8,128)(2,1)}, bf16[2,128,1024]{2,1,0:T(8,128)(2,1)}) custom-call(bf16[577,1024]{1,0:T(8,128)(2,1)} %get-tuple-element.295.refs_0_.refs_7_.x, bf16[4,577,1024]{2,1,0:T(8,128)(2,1)} %get-tuple-element.335.inner, ...), custom_call_target="tpu_custom_call" | custom-call | tf_op jit(solution)/shard_map/pallas_call | solution.py:142
  230.0 29.5 %shard_map.474 = (bf16[4,577,768]{2,1,0:T(8,128)(2,1)}, f32[4,2,256]{2,1,0:T(2,128)}, bf16[4,512,768]{2,1,0:T(8,128)(2,1)}) custom-call(bf16[577,1024]{1,0:T(8,128)(2,1)} %get-tuple-element.350.x.refs_0_, bf16[4,577,768]{2,1,0:T(8,128)(2,1)} %get-tuple-element.351.refs_1_, f32[4,8,577]{2,1,0:T(8,128)} %get-tuple-element.352.refs_2_, ...), custom_call_target="tpu_custom_call" | custom-call | tf_op jit(solution)/shard_map/pallas_call | solution.py:142
  271.1 4.9 %shard_map.475 = (bf16[4,128,256]{2,1,0:T(8,128)(2,1)}, bf16[4,128,256]{2,1,0:T(8,128)(2,1)}, bf16[4,128,256]{2,1,0:T(8,128)(2,1)}, bf16[2,128,256]{2,1,0:T(8,128)(2,1)}, bf16[2,128,256]{2,1,0:T(8,128)(2,1)}) custom-call(bf16[577,1024]{1,0:T(8,128)(2,1)} %get-tuple-element.350.x.refs_0_, bf16[4,577,256]{2,1,0:T(8,128)(2,1)} %get-tuple-element.361.refs_0_.inner, ...), custom_call_target="tpu_custom_call" | custom-call | tf_op jit(solution)/shard_map/pallas_call | solution.py:142
  277.7 6.9 %shard_map.476 = (bf16[4,128,768]{2,1,0:T(8,128)(2,1)}, bf16[4,128,768]{2,1,0:T(8,128)(2,1)}, bf16[4,128,768]{2,1,0:T(8,128)(2,1)}, bf16[2,128,768]{2,1,0:T(8,128)(2,1)}, bf16[2,128,768]{2,1,0:T(8,128)(2,1)}) custom-call(bf16[577,1024]{1,0:T(8,128)(2,1)} %get-tuple-element.369.refs_0_.refs_3_.x, bf16[4,577,768]{2,1,0:T(8,128)(2,1)} %get-tuple-element.377.inner.refs_0_, ...), custom_call_target="tpu_custom_call" | custom-call | tf_op jit(solution)/shard_map/pallas_call | solution.py:142
  287.1 11.8 %shard_map.477 = (f32[577,1024]{1,0:T(8,128)}, f32[2,1024]{1,0:T(2,128)}) custom-call(s32[8]{0:T(128)} %broadcast_xor_fusion.order, bf16[4,577,768]{2,1,0:T(8,128)(2,1)} %get-tuple-element.377.inner.refs_0_, f32[577,1024]{1,0:T(8,128)} %get-tuple-element.290.refs_1_, f32[577,1024]{1,0:T(8,128)} %get-tuple-element.378.refs_2_, ...), custom_call_target="tpu_custom_call" | custom-call | tf_op jit(solution)/shard_map/pallas_call | solution.py:142
  309.8 3.8 collective-permute-start.57
  321.2 12.2 %reduce-scatter.4.cloned.1.call-done = bf16[1,128,1024]{2,1,0:T(8,128)(2,1)} async-done(((bf16[4,128,1024]{2,1,0:T(8,128)(2,1)}), bf16[1,128,1024]{2,1,0:T(8,128)(2,1)}) %reduce-scatter.4.cloned.1.call-update) | async-done | bytes 262160 | tf_op jit(solution)/shard_map/reduce_scatter | solution.py:571
  344.2 4.4 %collective-permute-start.58 = (bf16[128,768]{1,0:T(8,128)(2,1)S(1)}, bf16[128,768]{1,0:T(8,128)(2,1)S(1)}, u32[]{:S(2)}, u32[]{:S(2)}) collective-permute-start(bf16[128,768]{1,0:T(8,128)(2,1)S(1)} %get-tuple-element.435), channel_id=1, source_target_pairs={{0,3},{1,0},{2,1},{3,2},{4,7},{5,4},{6,5},{7,6},{8,11},{9,8},{10,9... | collective-permute-start | bytes 589832 | tf_op jit(solution)/shard_map/ppermute | solution.py:523
  357.6 13.5 %reduce-scatter.8.cloned.1.call-done = bf16[1,128,256]{2,1,0:T(8,128)(2,1)} async-done(((bf16[4,128,256]{2,1,0:T(8,128)(2,1)}), bf16[1,128,256]{2,1,0:T(8,128)(2,1)}) %reduce-scatter.8.cloned.1.call-update) | async-done | bytes 65552 | tf_op jit(solution)/shard_map/reduce_scatter | solution.py:571
  (383 shorter events, 123.0 us)
Async XLA Ops:
  7.2 309.1 %reduce-scatter.6.cloned.1.call-start = ((), (), s32[]{:S(2)}) async-start(), calls=%async_computation.4 | async-start | bytes 1310720 | tf_op jit(solution)/shard_map/reduce_scatter | solution.py:571
  37.1 27.1 %collective-permute-start.3 = (bf16[4,128,1024]{2,1,0:T(8,128)(2,1)S(1)}, bf16[4,128,1024]{2,1,0:T(8,128)(2,1)S(1)}, u32[]{:S(2)}, u32[]{:S(2)}) collective-permute-start(bf16[4,128,1024]{2,1,0:T(8,128)(2,1)S(1)} %pad_maximum_fusion.refs_2_.refs_4_), channel_id=1, source_target_pairs={{0,8},{4,12},{8,0},{12,4},{16,24},{20,28},{24,16},{28,20},{1,9},{5... | collective-permute-start | bytes 3145736 | tf_op jit(solution)/shard_map/ppermute | solution.py:519
  38.6 25.6 %collective-permute-start.4 = (bf16[4,128,1024]{2,1,0:T(8,128)(2,1)S(1)}, bf16[4,128,1024]{2,1,0:T(8,128)(2,1)S(1)}, u32[]{:S(2)}, u32[]{:S(2)}) collective-permute-start(bf16[4,128,1024]{2,1,0:T(8,128)(2,1)S(1)} %pad_maximum_fusion.refs_2_.refs_4_), channel_id=1, source_target_pairs={{0,16},{4,20},{8,24},{12,28},{16,0},{20,4},{24,8},{28,12},{1,17},{... | collective-permute-start | bytes 3145736 | tf_op jit(solution)/shard_map/ppermute | solution.py:519
  79.6 32.7 %collective-permute-start.13 = (bf16[4,128,1024]{2,1,0:T(8,128)(2,1)S(1)}, bf16[4,128,1024]{2,1,0:T(8,128)(2,1)S(1)}, u32[]{:S(2)}, u32[]{:S(2)}) collective-permute-start(bf16[4,128,1024]{2,1,0:T(8,128)(2,1)S(1)} %pad_maximum_fusion.1.refs_3_.refs_18_), channel_id=1, source_target_pairs={{0,8},{4,12},{8,0},{12,4},{16,24},{20,28},{24,16},{28,20},{1,9},{5... | collective-permute-start | bytes 3145736 | tf_op jit(solution)/shard_map/ppermute | solution.py:519
  80.2 32.1 %collective-permute-start.14 = (bf16[4,128,1024]{2,1,0:T(8,128)(2,1)S(1)}, bf16[4,128,1024]{2,1,0:T(8,128)(2,1)S(1)}, u32[]{:S(2)}, u32[]{:S(2)}) collective-permute-start(bf16[4,128,1024]{2,1,0:T(8,128)(2,1)S(1)} %pad_maximum_fusion.1.refs_3_.refs_18_), channel_id=1, source_target_pairs={{0,16},{4,20},{8,24},{12,28},{16,0},{20,4},{24,8},{28,12},{1,17},{... | collective-permute-start | bytes 3145736 | tf_op jit(solution)/shard_map/ppermute | solution.py:519
  84.4 28.0 %collective-permute-start.17 = (bf16[128,1024]{1,0:T(8,128)(2,1)S(1)}, bf16[128,1024]{1,0:T(8,128)(2,1)}, u32[]{:S(2)}, u32[]{:S(2)}) collective-permute-start(bf16[128,1024]{1,0:T(8,128)(2,1)S(1)} %bitcast.80), channel_id=1, source_target_pairs={{0,1},{1,2},{2,3},{3,0},{4,5},{5,6},{6,7},{7,4},{8,9},{9,10},{10,1... | collective-permute-start | bytes 786440 | tf_op jit(solution)/shard_map/ppermute | solution.py:523
  129.4 24.5 %collective-permute-start.25 = (bf16[4,128,1024]{2,1,0:T(8,128)(2,1)S(1)}, bf16[4,128,1024]{2,1,0:T(8,128)(2,1)S(1)}, u32[]{:S(2)}, u32[]{:S(2)}) collective-permute-start(bf16[4,128,1024]{2,1,0:T(8,128)(2,1)S(1)} %pad_maximum_fusion.2.refs_8_), channel_id=1, source_target_pairs={{0,8},{4,12},{8,0},{12,4},{16,24},{20,28},{24,16},{28,20},{1,9},{5... | collective-permute-start | bytes 3145736 | tf_op jit(solution)/shard_map/ppermute | solution.py:519
  130.9 24.1 %collective-permute-start.26 = (bf16[4,128,1024]{2,1,0:T(8,128)(2,1)S(1)}, bf16[4,128,1024]{2,1,0:T(8,128)(2,1)S(1)}, u32[]{:S(2)}, u32[]{:S(2)}) collective-permute-start(bf16[4,128,1024]{2,1,0:T(8,128)(2,1)S(1)} %pad_maximum_fusion.2.refs_8_), channel_id=1, source_target_pairs={{0,16},{4,20},{8,24},{12,28},{16,0},{20,4},{24,8},{28,12},{1,17},{... | collective-permute-start | bytes 3145736 | tf_op jit(solution)/shard_map/ppermute | solution.py:519
  176.2 33.8 %collective-permute-start.37 = (bf16[2,128,1024]{2,1,0:T(8,128)(2,1)}, bf16[2,128,1024]{2,1,0:T(8,128)(2,1)S(1)}, u32[]{:S(2)}, u32[]{:S(2)}) collective-permute-start(bf16[2,128,1024]{2,1,0:T(8,128)(2,1)} %get-tuple-element.325), channel_id=1, source_target_pairs={{0,16},{4,20},{8,24},{12,28},{16,0},{20,4},{24,8},{28,12},{1,17},{... | collective-permute-start | bytes 1572872 | tf_op jit(solution)/shard_map/ppermute | solution.py:519
  177.0 33.0 %collective-permute-start.38 = (bf16[2,128,1024]{2,1,0:T(8,128)(2,1)}, bf16[2,128,1024]{2,1,0:T(8,128)(2,1)S(1)}, u32[]{:S(2)}, u32[]{:S(2)}) collective-permute-start(bf16[2,128,1024]{2,1,0:T(8,128)(2,1)} %get-tuple-element.326), channel_id=1, source_target_pairs={{0,8},{4,12},{8,0},{12,4},{16,24},{20,28},{24,16},{28,20},{1,9},{5... | collective-permute-start | bytes 1572872 | tf_op jit(solution)/shard_map/ppermute | solution.py:519
  215.2 44.3 %collective-permute-start.43 = (bf16[4,128,1024]{2,1,0:T(8,128)(2,1)S(1)}, bf16[4,128,1024]{2,1,0:T(8,128)(2,1)}, u32[]{:S(2)}, u32[]{:S(2)}) collective-permute-start(bf16[4,128,1024]{2,1,0:T(8,128)(2,1)S(1)} %pad_maximum_fusion.4), channel_id=1, source_target_pairs={{0,16},{4,20},{8,24},{12,28},{16,0},{20,4},{24,8},{28,12},{1,17},{... | collective-permute-start | bytes 3145736 | tf_op jit(solution)/shard_map/ppermute | solution.py:519
  216.6 42.9 %collective-permute-start.42 = (bf16[4,128,1024]{2,1,0:T(8,128)(2,1)S(1)}, bf16[4,128,1024]{2,1,0:T(8,128)(2,1)}, u32[]{:S(2)}, u32[]{:S(2)}) collective-permute-start(bf16[4,128,1024]{2,1,0:T(8,128)(2,1)S(1)} %pad_maximum_fusion.3), channel_id=1, source_target_pairs={{0,8},{4,12},{8,0},{12,4},{16,24},{20,28},{24,16},{28,20},{1,9},{5... | collective-permute-start | bytes 3145736 | tf_op jit(solution)/shard_map/ppermute | solution.py:519
  227.6 32.0 %collective-permute-start.44 = (bf16[4,512,256]{2,1,0:T(8,128)(2,1)S(1)}, bf16[4,512,256]{2,1,0:T(8,128)(2,1)S(1)}, u32[]{:S(2)}, u32[]{:S(2)}) collective-permute-start(bf16[4,512,256]{2,1,0:T(8,128)(2,1)S(1)} %copy-done.33), channel_id=1, source_target_pairs={{0,4},{4,0},{8,12},{12,8},{16,20},{20,16},{24,28},{28,24},{1,5},{5... | collective-permute-start | bytes 3145736 | tf_op jit(solution)/shard_map/ppermute | solution.py:519
  227.7 31.8 %collective-permute-start.40 = (bf16[2,128,1024]{2,1,0:T(8,128)(2,1)}, bf16[2,128,1024]{2,1,0:T(8,128)(2,1)S(1)}, u32[]{:S(2)}, u32[]{:S(2)}) collective-permute-start(bf16[2,128,1024]{2,1,0:T(8,128)(2,1)} %get-tuple-element.344), channel_id=1, source_target_pairs={{0,16},{4,20},{8,24},{12,28},{16,0},{20,4},{24,8},{28,12},{1,17},{... | collective-permute-start | bytes 1572872 | tf_op jit(solution)/shard_map/ppermute | solution.py:519
  228.7 30.9 %collective-permute-start.41 = (bf16[2,128,1024]{2,1,0:T(8,128)(2,1)}, bf16[2,128,1024]{2,1,0:T(8,128)(2,1)}, u32[]{:S(2)}, u32[]{:S(2)}) collective-permute-start(bf16[2,128,1024]{2,1,0:T(8,128)(2,1)} %get-tuple-element.345), channel_id=1, source_target_pairs={{0,8},{4,12},{8,0},{12,4},{16,24},{20,28},{24,16},{28,20},{1,9},{5... | collective-permute-start | bytes 1572872 | tf_op jit(solution)/shard_map/ppermute | solution.py:519
  264.4 35.5 %collective-permute-start.49 = (bf16[4,128,1024]{2,1,0:T(8,128)(2,1)}, bf16[4,128,1024]{2,1,0:T(8,128)(2,1)}, u32[]{:S(2)}, u32[]{:S(2)}) collective-permute-start(bf16[4,128,1024]{2,1,0:T(8,128)(2,1)} %pad_maximum_fusion.6), channel_id=1, source_target_pairs={{0,16},{4,20},{8,24},{12,28},{16,0},{20,4},{24,8},{28,12},{1,17},{... | collective-permute-start | bytes 3145736 | tf_op jit(solution)/shard_map/ppermute | solution.py:519
  266.7 33.2 %collective-permute-start.48 = (bf16[4,128,1024]{2,1,0:T(8,128)(2,1)}, bf16[4,128,1024]{2,1,0:T(8,128)(2,1)}, u32[]{:S(2)}, u32[]{:S(2)}) collective-permute-start(bf16[4,128,1024]{2,1,0:T(8,128)(2,1)} %pad_maximum_fusion.5), channel_id=1, source_target_pairs={{0,8},{4,12},{8,0},{12,4},{16,24},{20,28},{24,16},{28,20},{1,9},{5... | collective-permute-start | bytes 3145736 | tf_op jit(solution)/shard_map/ppermute | solution.py:519
  271.0 62.4 %reduce-scatter.4.cloned.1.call-start = ((), (), s32[]{:S(2)}) async-start(), calls=%async_computation.3 | async-start | bytes 1310720 | tf_op jit(solution)/shard_map/reduce_scatter | solution.py:571
  305.5 65.6 %reduce-scatter.8.cloned.1.call-start = ((), (), s32[]{:S(2)}) async-start(), calls=%async_computation.5 | async-start | bytes 327680 | tf_op jit(solution)/shard_map/reduce_scatter | solution.py:571
  307.5 27.5 %collective-permute-start.50 = (bf16[4,128,768]{2,1,0:T(8,128)(2,1)S(1)}, bf16[4,128,768]{2,1,0:T(8,128)(2,1)}, u32[]{:S(2)}, u32[]{:S(2)}) collective-permute-start(bf16[4,128,768]{2,1,0:T(8,128)(2,1)S(1)} %pad_maximum_fusion.9), channel_id=1, source_target_pairs={{0,8},{4,12},{8,0},{12,4},{16,24},{20,28},{24,16},{28,20},{1,9},{5... | collective-permute-start | bytes 2359304 | tf_op jit(solution)/shard_map/ppermute | solution.py:519
  308.9 26.1 %collective-permute-start.51 = (bf16[4,128,768]{2,1,0:T(8,128)(2,1)S(1)}, bf16[4,128,768]{2,1,0:T(8,128)(2,1)}, u32[]{:S(2)}, u32[]{:S(2)}) collective-permute-start(bf16[4,128,768]{2,1,0:T(8,128)(2,1)S(1)} %pad_maximum_fusion.10), channel_id=1, source_target_pairs={{0,16},{4,20},{8,24},{12,28},{16,0},{20,4},{24,8},{28,12},{1,17},{... | collective-permute-start | bytes 2359304 | tf_op jit(solution)/shard_map/ppermute | solution.py:519
  344.2 30.4 %collective-permute-start.58 = (bf16[128,768]{1,0:T(8,128)(2,1)S(1)}, bf16[128,768]{1,0:T(8,128)(2,1)S(1)}, u32[]{:S(2)}, u32[]{:S(2)}) collective-permute-start(bf16[128,768]{1,0:T(8,128)(2,1)S(1)} %get-tuple-element.435), channel_id=1, source_target_pairs={{0,3},{1,0},{2,1},{3,2},{4,7},{5,4},{6,5},{7,6},{8,11},{9,8},{10,9... | collective-permute-start | bytes 589832 | tf_op jit(solution)/shard_map/ppermute | solution.py:523
  348.6 25.9 %collective-permute-start.59 = (bf16[128,768]{1,0:T(8,128)(2,1)S(1)}, bf16[128,768]{1,0:T(8,128)(2,1)S(1)}, u32[]{:S(2)}, u32[]{:S(2)}) collective-permute-start(bf16[128,768]{1,0:T(8,128)(2,1)S(1)} %get-tuple-element.436), channel_id=1, source_target_pairs={{0,2},{1,3},{2,0},{3,1},{4,6},{5,7},{6,4},{7,5},{8,10},{9,11},{10,... | collective-permute-start | bytes 589832 | tf_op jit(solution)/shard_map/ppermute | solution.py:523
  349.4 25.1 %collective-permute-start.60 = (bf16[128,768]{1,0:T(8,128)(2,1)S(1)}, bf16[128,768]{1,0:T(8,128)(2,1)}, u32[]{:S(2)}, u32[]{:S(2)}) collective-permute-start(bf16[128,768]{1,0:T(8,128)(2,1)S(1)} %get-tuple-element.437), channel_id=1, source_target_pairs={{0,1},{1,2},{2,3},{3,0},{4,5},{5,6},{6,7},{7,4},{8,9},{9,10},{10,1... | collective-permute-start | bytes 589832 | tf_op jit(solution)/shard_map/ppermute | solution.py:523
  (122 other events, 1370.7 us)
Sparse Core Ops, SparseCore 0:
  271.1 28.0 reduce-scatter.5
  305.6 27.7 reduce-scatter.3
  344.3 26.7 reduce-scatter.7
